TPU v7x, 512 devices: a whole 4x8x8 slice. The times are simulated.
512 devices in a mesh: branch: 4 (over z_hi), row: 16 (over y, core), col: 8 (over z_lo, x).
Axes of the slice: x: 4, y: 8, z: 8 (z_hi: 4, z_lo: 2; z = z_hi * 2 + z_lo), core: 2. Of those that a mesh axis runs over, the one named last changes fastest.
Arguments:
- homolog_tensor: bfloat16 [256, 128, 256], P('col', 'row'), may hold values from -6 to 6
- couple_tensor: bfloat16 [128, 128, 128], P('row', 'col'), may hold values from -6 to 6
- probe_matrix: bfloat16 [256, 256], P(None, 'branch'), may hold values from -0.375 to 0.375
- lookup_matrix: bfloat16 [256, 256], P(None, 'branch'), may hold values from -0.375 to 0.375
- content_matrix: bfloat16 [256, 256], P(None, 'branch'), may hold values from -0.375 to 0.375
- scoring_sigmoid_matrix: bfloat16 [256, 256], P(None, 'branch'), may hold values from -0.375 to 0.375
- scoring_final_matrix: bfloat16 [256, 256], P('branch'), may hold values from -0.375 to 0.375
- couple_offset_matrix: bfloat16 [128, 8], P(None, 'branch'), may hold values from -43 to 43
- product_first_matrix: bfloat16 [256, 32], replicated, may hold values from -0.375 to 0.375
- product_second_matrix: bfloat16 [256, 32], replicated, may hold values from -0.375 to 0.375
- product_final_matrix: bfloat16 [1024, 128], replicated, may hold values from -1 to 1
- trio_first_matrix: bfloat16 [2, 128, 128], P(None, None, 'branch'), may hold values from -0.5 to 0.5
- trio_second_matrix: bfloat16 [2, 128, 128], P(None, None, 'branch'), may hold values from -0.5 to 0.5
- trio_sigmoid_matrix: bfloat16 [128, 128], replicated, may hold values from -0.5 to 0.5
- trio_final_matrix: bfloat16 [128, 128], replicated, may hold values from -0.5 to 0.5
Outputs:
- revised_homolog_matrix: bfloat16 [256, 128, 256], P('col', 'row', 'branch')
- pairwise_output: bfloat16 [128, 128, 128], P('row', 'col')
All inputs are finite; a program needn't handle non-finite values.
Results may differ from a plain program's by a relative error of at most 0.014.
Values may be sent and summed in bfloat16 or wider, within the bound.
A program may use at most 64 MiB of HBM per device.

v0:
```python
import jax
import jax.numpy as jnp
from jax import lax
from jax.sharding import PartitionSpec as P

EPS = 1e-05


def in_order(pieces, dim):
    shape = list(pieces.shape[1:])
    shape[dim] *= pieces.shape[0]
    return jnp.moveaxis(pieces, 0, dim).reshape(shape)


def sent_to_all(array, axis):
    copies = jnp.broadcast_to(array, (lax.axis_size(axis), *array.shape))
    return lax.all_to_all(copies, axis, split_axis=0, concat_axis=0, tiled=True)


def gathered_copies(array, axis, dim):
    return in_order(sent_to_all(array, axis), dim)


def side_by_side(arrays, axis, dim, along):
    widths = [a.shape[along] for a in arrays]
    both = jnp.concatenate(arrays, axis=along)
    result = lax.all_gather(both, axis, axis=dim, tiled=True)
    return tuple(jnp.split(result, [sum(widths[:k]) for k in range(1, len(widths))], axis=along))


def in_blocks(array, dim, length):
    before, after = (array.shape[:dim], array.shape[dim + 1 :])
    return jnp.moveaxis(array.reshape(*before, length, -1, *after), dim, 0)


def summed_on_arrival(array, axis, dim):
    length = lax.axis_size(axis)
    pieces = lax.all_to_all(in_blocks(array, dim, length), axis, 0, 0, tiled=True)
    return jnp.sum(pieces.astype(jnp.float32), axis=0)


def from_root(array, axis, root):
    return lax.dynamic_index_in_dim(lax.all_gather(array, axis), root, 0, keepdims=False)


def standardise_rows(values):
    values = values.astype(jnp.float32)
    centred = values - jnp.mean(values, axis=-1, keepdims=True)
    variance = jnp.mean(centred * centred, axis=-1, keepdims=True)
    return centred / jnp.sqrt(variance + EPS)


def apply_linear(source, weights):
    return jnp.dot(
        source.reshape(-1, weights.shape[0]), weights, preferred_element_type=jnp.float32
    )


def attend(query, key, value, bias):
    scale = float(query.shape[-1]) ** (-0.5)
    scores = jnp.einsum("sihd,sjhd->shij", query, key, preferred_element_type=jnp.float32) * scale
    scores = scores + jnp.transpose(bias, (2, 0, 1)).astype(jnp.float32)[None]
    top = jnp.max(scores, axis=-1, keepdims=True)
    expo = jnp.exp(scores - top)
    total = jnp.sum(expo, axis=-1)
    summed = jnp.einsum(
        "shij,sjhd->sihd", expo.astype(jnp.bfloat16), value, preferred_element_type=jnp.float32
    )
    return summed / jnp.transpose(total, (0, 2, 1))[..., None]


def per_device(
    homolog_tensor,
    couple_tensor,
    probe_matrix,
    lookup_matrix,
    content_matrix,
    scoring_sigmoid_matrix,
    scoring_final_matrix,
    couple_offset_matrix,
    product_first_matrix,
    product_second_matrix,
    product_final_matrix,
    trio_first_matrix,
    trio_second_matrix,
    trio_sigmoid_matrix,
    trio_final_matrix,
):
    branches = lax.axis_size("branch")
    rows_count = lax.axis_size("row")
    cols_count = lax.axis_size("col")
    quadrant_share = lax.axis_index("branch")
    col_index = lax.axis_index("col")
    homolog_share, position_tile, channel_extent = homolog_tensor.shape
    c_block = couple_tensor.shape[1]
    depth = probe_matrix.shape[1]
    local_heads = couple_offset_matrix.shape[1]
    head_size = depth // local_heads
    q_rows = position_tile // branches
    total_rows = homolog_share * cols_count
    outer_width = product_first_matrix.shape[1]
    standardised_tensor = standardise_rows(homolog_tensor).astype(jnp.bfloat16)
    pair_normed = standardise_rows(couple_tensor).astype(jnp.bfloat16)
    bias_tile = (
        apply_linear(pair_normed, couple_offset_matrix)
        .astype(jnp.bfloat16)
        .reshape(position_tile, c_block, local_heads)
    )
    bias_band = gathered_copies(bias_tile, "col", 1)
    shaped = (homolog_share, position_tile, local_heads, head_size)
    query = apply_linear(standardised_tensor, probe_matrix).astype(jnp.bfloat16).reshape(shaped)
    key = apply_linear(standardised_tensor, lookup_matrix).astype(jnp.bfloat16).reshape(shaped)
    value = apply_linear(standardised_tensor, content_matrix).astype(jnp.bfloat16).reshape(shaped)
    gate_pre = apply_linear(standardised_tensor, scoring_sigmoid_matrix).reshape(shaped)
    key_all, value_all = side_by_side((key, value), "row", 1, 0)
    attended_values = attend(query, key_all, value_all, bias_band) * jax.nn.sigmoid(gate_pre)
    attended_values = attended_values.astype(jnp.bfloat16).reshape(
        homolog_share, position_tile, depth
    )
    joined_tensor = apply_linear(attended_values, scoring_final_matrix).reshape(
        homolog_share, position_tile, channel_extent
    )
    joined_tensor = summed_on_arrival(joined_tensor.astype(jnp.bfloat16), "branch", 2)
    device_share = channel_extent // branches
    local_alignment = lax.dynamic_slice_in_dim(
        homolog_tensor, quadrant_share * device_share, device_share, 2
    )
    revised_homolog_matrix = (local_alignment.astype(jnp.float32) + joined_tensor).astype(
        jnp.bfloat16
    )
    left_rows = lax.dynamic_slice_in_dim(standardised_tensor, quadrant_share * q_rows, q_rows, 1)
    left_outer = (
        apply_linear(left_rows, product_first_matrix)
        .astype(jnp.bfloat16)
        .reshape(homolog_share, q_rows * outer_width)
    )
    right_local = (
        apply_linear(standardised_tensor, product_second_matrix)
        .astype(jnp.bfloat16)
        .reshape(homolog_share, position_tile, outer_width)
    )
    right_outer = gathered_copies(right_local, "row", 1)
    wide_out = product_final_matrix.astype(jnp.float32)
    left_major = jnp.transpose(left_outer)
    count = c_block * lax.axis_size("col")
    piece = right_outer.reshape(homolog_share, count * outer_width)
    outer = jnp.dot(left_major, piece, preferred_element_type=jnp.float32)
    outer = outer.reshape(q_rows, outer_width, count, outer_width)
    outer = jnp.transpose(outer, (2, 0, 1, 3)).reshape(count * q_rows, outer_width * outer_width)
    term = jnp.dot(outer, wide_out) / total_rows
    update = summed_on_arrival(
        term.reshape(count, q_rows, wide_out.shape[1]).astype(jnp.bfloat16), "col", 0
    )
    update = jnp.transpose(update, (1, 0, 2))
    pair_rows = lax.dynamic_slice_in_dim(couple_tensor, quadrant_share * q_rows, q_rows, 0)
    mid_rows = (pair_rows.astype(jnp.float32) + update).astype(jnp.bfloat16)
    pair_mid = gathered_copies(mid_rows, "branch", 0)
    tri_normed = standardise_rows(pair_mid).astype(jnp.bfloat16)

    def gated(weights):
        linear = apply_linear(tri_normed, weights[0])
        opening = apply_linear(tri_normed, weights[1])
        return (
            (jax.nn.sigmoid(opening) * linear)
            .astype(jnp.bfloat16)
            .reshape(position_tile, c_block, weights.shape[2])
        )

    tri_left = gated(trio_first_matrix)
    tri_right = gated(trio_second_matrix)
    left_band, right_band = side_by_side((tri_left, tri_right), "col", 1, 0)
    ratio = rows_count // cols_count

    def mirror(offset):
        return from_root(right_band, "row", col_index * ratio + offset)

    right_cols = jnp.concatenate([mirror(offset) for offset in range(ratio)], axis=0)
    product = jnp.einsum("ikc,jkc->ijc", left_band, right_cols, preferred_element_type=jnp.float32)
    product = lax.all_to_all(product, "branch", split_axis=0, concat_axis=2, tiled=True)
    product_normed = standardise_rows(product).astype(jnp.bfloat16)
    own_normed = lax.dynamic_slice_in_dim(tri_normed, quadrant_share * q_rows, q_rows, 0)
    closing = jax.nn.sigmoid(apply_linear(own_normed, trio_sigmoid_matrix)).reshape(
        q_rows, c_block, -1
    )
    change = apply_linear(product_normed, trio_final_matrix).reshape(q_rows, c_block, -1)
    out_rows = (mid_rows.astype(jnp.float32) + closing * change).astype(jnp.bfloat16)
    pairwise_output = gathered_copies(out_rows, "branch", 0)
    return (revised_homolog_matrix, pairwise_output)


def solution(mesh):
    return jax.shard_map(
        per_device,
        mesh=mesh,
        in_specs=(
            P("col", "row", None),
            P("row", "col", None),
            P(None, "branch"),
            P(None, "branch"),
            P(None, "branch"),
            P(None, "branch"),
            P("branch", None),
            P(None, "branch"),
            P(),
            P(),
            P(),
            P(None, None, "branch"),
            P(None, None, "branch"),
            P(),
            P(),
        ),
        out_specs=(P("col", "row", "branch"), P("row", "col", None)),
        check_vma=False,
    )
```

profile of v0, /device:TPU:1, one launch (start us, length us, event | category | flops | bytes accessed | tf_op | source)
XLA Modules:
  0.0 188.8 jit_solution(8965825571043323615)
XLA Ops:
  7.2 1.1 convert_reduce_fusion.1
  8.3 1.1 fusion.23
  9.4 1.0 fusion.24
  10.4 0.9 convolution_convert_fusion.4
  11.5 0.2 broadcast_in_dim.9
  11.7 1.7 reshape.245
  13.4 10.2 %all-to-all-start.2 = ((bf16[16,2,4096]{2,1,0:T(2,128)(2,1)}), bf16[16,2,4096]{2,1,0:T(2,128)(2,1)S(1)}, u32[]{:S(2)}, u32[]{:S(2)}) async-start(bf16[16,2,4096]{2,1,0:T(2,128)(2,1)} %reshape.245), calls=%async_computation.2 | async-start | bytes 524288 | tf_op jit(solution)/shard_map/all_to_all | solution.py:17
  24.1 0.2 copy.92
  24.7 0.2 copy.93
  24.9 0.8 pad_maximum_fusion
  25.9 0.2 fusion.41
  26.8 0.7 reshape.241
  27.5 1.0 fusion.5
  28.5 7.0 %all-to-all-done.2 = bf16[16,2,4096]{2,1,0:T(2,128)(2,1)S(1)} async-done(((bf16[16,2,4096]{2,1,0:T(2,128)(2,1)}), bf16[16,2,4096]{2,1,0:T(2,128)(2,1)S(1)}, u32[]{:S(2)}, u32[]{:S(2)}) %all-to-all-start.2) | async-done | bytes 262176 | tf_op jit(solution)/shard_map/all_to_all | solution.py:17
  35.5 4.1 %all-to-all-start = ((bf16[8,2,128]{2,1,0:T(2,128)(2,1)}), bf16[8,2,128]{2,1,0:T(2,128)(2,1)S(1)}, u32[]{:S(2)}, u32[]{:S(2)}) async-start(bf16[8,2,128]{2,1,0:T(2,128)(2,1)} %reshape.241), calls=%async_computation | async-start | bytes 8192 | tf_op jit(solution)/shard_map/all_to_all | solution.py:17
  39.6 0.5 reshape.246
  40.1 0.3 copy.103
  40.4 1.1 reshape_reshape.4
  41.5 0.8 dot_general.87
  42.3 0.5 copy.105
  42.8 0.3 convolution_bitcast_fusion
  43.1 3.2 %copy.106 = bf16[128,2,32,32]{3,2,1,0:T(8,128)(2,1)S(1)} copy(bf16[128,2,32,32]{0,2,3,1:T(8,128)(2,1)S(1)} %convolution_bitcast_fusion) | data formatting | bytes 1048576 | tf_op jit(solution)/shard_map/transpose | solution.py:149
  46.4 2.2 %reshape.226 = bf16[256,1024]{1,0:T(8,128)(2,1)S(1)} reshape(bf16[128,2,32,32]{3,2,1,0:T(8,128)(2,1)S(1)} %copy.106) | data formatting | bytes 1048576 | tf_op jit(solution)/shard_map/reshape | solution.py:149
  48.6 0.9 fusion.7
  49.5 5.2 %all-to-all-start.3 = ((bf16[8,16,2,128]{3,2,1,0:T(2,128)(2,1)}), bf16[8,16,2,128]{3,2,1,0:T(2,128)(2,1)S(1)}, u32[]{:S(2)}, u32[]{:S(2)}) async-start(bf16[8,16,2,128]{3,2,1,0:T(2,128)(2,1)} %bitcast.22), calls=%async_computation.3 | async-start | bytes 131072 | tf_op jit(solution)/shard_map/all_to_all | solution.py:38
  55.2 4.8 %all-to-all-done.3 = bf16[8,16,2,128]{3,2,1,0:T(2,128)(2,1)S(1)} async-done(((bf16[8,16,2,128]{3,2,1,0:T(2,128)(2,1)}), bf16[8,16,2,128]{3,2,1,0:T(2,128)(2,1)S(1)}, u32[]{:S(2)}, u32[]{:S(2)}) %all-to-all-start.3) | async-done | bytes 65568 | tf_op jit(solution)/shard_map/all_to_all | solution.py:38
  60.1 0.6 broadcast_in_dim.10
  60.7 9.1 %all-to-all-start.4 = ((bf16[4,2,16,128]{3,2,1,0:T(8,128)(2,1)}), bf16[4,2,16,128]{3,2,1,0:T(8,128)(2,1)S(1)}, u32[]{:S(2)}, u32[]{:S(2)}) async-start(bf16[4,2,16,128]{3,2,1,0:T(8,128)(2,1)} %broadcast_in_dim.10), calls=%async_computation.4 | async-start | bytes 65536 | tf_op jit(solution)/shard_map/all_to_all | solution.py:17
  69.9 6.6 %all-to-all-done.4 = bf16[4,2,16,128]{3,2,1,0:T(8,128)(2,1)S(1)} async-done(((bf16[4,2,16,128]{3,2,1,0:T(8,128)(2,1)}), bf16[4,2,16,128]{3,2,1,0:T(8,128)(2,1)S(1)}, u32[]{:S(2)}, u32[]{:S(2)}) %all-to-all-start.4) | async-done | bytes 32800 | tf_op jit(solution)/shard_map/all_to_all | solution.py:17
  76.6 0.2 multiply_reduce_fusion.1
  77.4 0.2 fusion.11
  77.9 23.6 %all_gather.15 = bf16[16,128,32]{2,0,1:T(8,128)(2,1)S(1)} all-gather(bf16[16,16,32]{2,0,1:T(8,128)(2,1)S(1)} %copy.110), channel_id=1, replica_groups=mesh['branch'=4,'row'=16,'col'=8] {'col'}, dimensions={1}, use_global_device_ids=true | all-gather | bytes 147456 | tf_op jit(solution)/shard_map/all_gather | solution.py:27
  101.4 0.8 fusion.60
  102.2 0.8 copy.123
  103.1 0.7 fusion.46
  103.8 4.6 %fusion.59 = (bf16[32,128,2,32]{0,3,2,1:T(8,128)(2,1)}, bf16[32,128,2,32]{0,3,2,1:T(8,128)(2,1)S(1)}) fusion(bf16[64,128,2,32]{0,3,2,1:T(8,128)(2,1)} %all-gather.4.cloned.1.call-done), kind=kLoop, calls=%fused_computation.109 | loop fusion | bytes 2097152 | tf_op jit(solution)/shard_map/split | solution.py:28
  108.4 4.1 %copy.120 = bf16[32,128,2,32]{1,3,2,0:T(8,128)(2,1)S(1)} copy(bf16[32,128,2,32]{0,3,2,1:T(8,128)(2,1)} %get-tuple-element.4) | data formatting | bytes 1048576
  112.4 2.6 %copy.119 = bf16[32,128,2,32]{1,3,2,0:T(8,128)(2,1)S(1)} copy(bf16[32,128,2,32]{0,3,2,1:T(8,128)(2,1)S(1)} %get-tuple-element.5) | data formatting | bytes 1048576
  115.1 0.4 fusion.61
  115.4 0.3 fusion.26
  115.7 1.4 fusion.6
  117.4 0.2 convolution_convert_fusion
  117.6 0.2 reshape.222
  117.8 0.9 reshape.243
  118.7 3.5 %all-to-all-start.1 = ((bf16[4,2,8192]{2,1,0:T(2,128)(2,1)}), bf16[4,2,8192]{2,1,0:T(2,128)(2,1)S(1)}, u32[]{:S(2)}, u32[]{:S(2)}) async-start(bf16[4,2,8192]{2,1,0:T(2,128)(2,1)} %reshape.243), calls=%async_computation.1 | async-start | bytes 262144 | tf_op jit(solution)/shard_map/all_to_all | solution.py:38
  122.3 7.0 %all-to-all-done.1 = bf16[4,2,8192]{2,1,0:T(2,128)(2,1)S(1)} async-done(((bf16[4,2,8192]{2,1,0:T(2,128)(2,1)}), bf16[4,2,8192]{2,1,0:T(2,128)(2,1)S(1)}, u32[]{:S(2)}, u32[]{:S(2)}) %all-to-all-start.1) | async-done | bytes 131104 | tf_op jit(solution)/shard_map/all_to_all | solution.py:38
  129.4 0.2 reshape.244
  129.6 24.7 %all-gather.6.cloned.1.call-done = bf16[128,128,32]{2,0,1:T(8,128)(2,1)} async-done(((bf16[8,128,32]{2,0,1:T(8,128)(2,1)}), bf16[128,128,32]{2,0,1:T(8,128)(2,1)}) %all-gather.6.cloned.1.call-update) | async-done | bytes 1048592 | tf_op jit(solution)/shard_map/all_gather | solution.py:43
  154.3 1.1 constant_dynamic-slice_fusion.2
  155.4 0.2 copy.121
  155.6 0.2 copy.122
  155.8 0.2 convolution_bitcast_fusion.2
  156.1 0.7 reshape.247
  156.8 5.4 %all-to-all-start.5 = ((f32[4,1,1024]{2,1,0:T(1,128)}), f32[4,1,1024]{2,1,0:T(1,128)S(1)}, u32[]{:S(2)}, u32[]{:S(2)}) async-start(f32[4,1,1024]{2,1,0:T(1,128)} %reshape.247), calls=%async_computation.5 | async-start | bytes 32768 | tf_op jit(solution)/shard_map/all_to_all | solution.py:179
  162.3 6.6 %all-to-all-done.5 = f32[4,1,1024]{2,1,0:T(1,128)S(1)} async-done(((f32[4,1,1024]{2,1,0:T(1,128)}), f32[4,1,1024]{2,1,0:T(1,128)S(1)}, u32[]{:S(2)}, u32[]{:S(2)}) %all-to-all-start.5) | async-done | bytes 16416 | tf_op jit(solution)/shard_map/all_to_all | solution.py:179
  168.8 0.5 broadcast.154
  169.4 0.7 reduce.4
  170.3 0.2 multiply_reduce_fusion
  170.6 0.2 fusion.20
  170.8 0.6 broadcast_in_dim.11
  171.4 3.3 %all-to-all-start.6 = ((bf16[4,2,16,128]{3,2,1,0:T(8,128)(2,1)}), bf16[4,2,16,128]{3,2,1,0:T(8,128)(2,1)S(1)}, u32[]{:S(2)}, u32[]{:S(2)}) async-start(bf16[4,2,16,128]{3,2,1,0:T(8,128)(2,1)} %broadcast_in_dim.11), calls=%async_computation.6 | async-start | bytes 65536 | tf_op jit(solution)/shard_map/all_to_all | solution.py:17
  174.7 0.7 add_convert_fusion
  175.4 5.9 %all-to-all-done.6 = bf16[4,2,16,128]{3,2,1,0:T(8,128)(2,1)S(1)} async-done(((bf16[4,2,16,128]{3,2,1,0:T(8,128)(2,1)}), bf16[4,2,16,128]{3,2,1,0:T(8,128)(2,1)S(1)}, u32[]{:S(2)}, u32[]{:S(2)}) %all-to-all-start.6) | async-done | bytes 32800 | tf_op jit(solution)/shard_map/all_to_all | solution.py:17
  181.4 0.6 copy.132
  (94 shorter events, 4.6 us)
Async XLA Ops:
  7.2 41.5 %copy-start = (bf16[1024,128]{1,0:T(8,128)(2,1)S(1)}, bf16[1024,128]{1,0:T(8,128)(2,1)}, u32[]{:S(2)}) copy-start(bf16[1024,128]{1,0:T(8,128)(2,1)} %param.25) | copy-start | bytes 786436
  7.2 16.5 %copy-start.5 = (bf16[256,64]{0,1:T(8,128)(2,1)S(1)}, bf16[256,64]{0,1:T(8,128)(2,1)}, u32[]{:S(2)}) copy-start(bf16[256,64]{0,1:T(8,128)(2,1)} %param.18) | copy-start | bytes 98308
  9.4 14.9 %copy-start.6 = (bf16[256,64]{0,1:T(8,128)(2,1)S(1)}, bf16[256,64]{0,1:T(8,128)(2,1)}, u32[]{:S(2)}) copy-start(bf16[256,64]{0,1:T(8,128)(2,1)} %param.19) | copy-start | bytes 98308
  11.7 14.1 %copy-start.2 = (bf16[8,16,128]{2,1,0:T(8,128)(2,1)S(1)}, bf16[8,16,128]{2,1,0:T(8,128)(2,1)}, u32[]{:S(2)}) copy-start(bf16[8,16,128]{2,1,0:T(8,128)(2,1)} %param.16) | copy-start | bytes 98308
  11.7 14.5 %copy-start.8 = (bf16[256,32]{0,1:T(8,128)(2,1)S(1)}, bf16[256,32]{0,1:T(8,128)(2,1)}, u32[]{:S(2)}) copy-start(bf16[256,32]{0,1:T(8,128)(2,1)} %param.23) | copy-start | bytes 49156
  11.7 14.6 %copy-start.12 = (bf16[128,2]{0,1:T(2,128)(2,1)S(1)}, bf16[128,2]{0,1:T(2,128)(2,1)}, u32[]{:S(2)}) copy-start(bf16[128,2]{0,1:T(2,128)(2,1)} %param.22) | copy-start | bytes 1540
  11.7 15.8 %copy-start.13 = (bf16[256,64]{0,1:T(8,128)(2,1)S(1)}, bf16[256,64]{0,1:T(8,128)(2,1)}, u32[]{:S(2)}) copy-start(bf16[256,64]{0,1:T(8,128)(2,1)} %param.20) | copy-start | bytes 98308
  13.4 22.1 %all-to-all-start.2 = ((bf16[16,2,4096]{2,1,0:T(2,128)(2,1)}), bf16[16,2,4096]{2,1,0:T(2,128)(2,1)S(1)}, u32[]{:S(2)}, u32[]{:S(2)}) async-start(bf16[16,2,4096]{2,1,0:T(2,128)(2,1)} %reshape.245), calls=%async_computation.2 | async-start | bytes 524288 | tf_op jit(solution)/shard_map/all_to_all | solution.py:17
  23.6 80.1 %all-gather.4.cloned.1.call-start = ((), (), s32[]{:S(2)}) async-start(), calls=%async_computation.7 | async-start | bytes 2228224 | tf_op jit(solution)/shard_map/all_gather | solution.py:27
  35.5 14.1 %all-to-all-start = ((bf16[8,2,128]{2,1,0:T(2,128)(2,1)}), bf16[8,2,128]{2,1,0:T(2,128)(2,1)S(1)}, u32[]{:S(2)}, u32[]{:S(2)}) async-start(bf16[8,2,128]{2,1,0:T(2,128)(2,1)} %reshape.241), calls=%async_computation | async-start | bytes 8192 | tf_op jit(solution)/shard_map/all_to_all | solution.py:17
  46.3 8.4 %copy-start.7 = (bf16[256,64]{0,1:T(8,128)(2,1)S(1)}, bf16[256,64]{0,1:T(8,128)(2,1)}, u32[]{:S(2)}) copy-start(bf16[256,64]{0,1:T(8,128)(2,1)} %param.17) | copy-start | bytes 98308
  46.4 30.6 %copy-start.10 = (bf16[2,128,32]{1,2,0:T(8,128)(2,1)S(1)}, bf16[2,128,32]{1,2,0:T(8,128)(2,1)}, u32[]{:S(2)}) copy-start(bf16[2,128,32]{1,2,0:T(8,128)(2,1)} %param.26) | copy-start | bytes 49156
  46.4 31.0 %copy-start.11 = (bf16[2,128,32]{1,2,0:T(8,128)(2,1)S(1)}, bf16[2,128,32]{1,2,0:T(8,128)(2,1)}, u32[]{:S(2)}) copy-start(bf16[2,128,32]{1,2,0:T(8,128)(2,1)} %param.27) | copy-start | bytes 49156
  49.5 10.4 %all-to-all-start.3 = ((bf16[8,16,2,128]{3,2,1,0:T(2,128)(2,1)}), bf16[8,16,2,128]{3,2,1,0:T(2,128)(2,1)S(1)}, u32[]{:S(2)}, u32[]{:S(2)}) async-start(bf16[8,16,2,128]{3,2,1,0:T(2,128)(2,1)} %bitcast.22), calls=%async_computation.3 | async-start | bytes 131072 | tf_op jit(solution)/shard_map/all_to_all | solution.py:38
  60.7 15.8 %all-to-all-start.4 = ((bf16[4,2,16,128]{3,2,1,0:T(8,128)(2,1)}), bf16[4,2,16,128]{3,2,1,0:T(8,128)(2,1)S(1)}, u32[]{:S(2)}, u32[]{:S(2)}) async-start(bf16[4,2,16,128]{3,2,1,0:T(8,128)(2,1)} %broadcast_in_dim.10), calls=%async_computation.4 | async-start | bytes 65536 | tf_op jit(solution)/shard_map/all_to_all | solution.py:17
  69.8 84.5 %all-gather.6.cloned.1.call-start = ((), (), s32[]{:S(2)}) async-start(), calls=%async_computation.8 | async-start | bytes 4456448 | tf_op jit(solution)/shard_map/all_gather | solution.py:43
  115.7 1.7 copy-start.4
  117.2 5.0 %copy-start.9 = (bf16[2,16,128]{2,1,0:T(8,128)(2,1)S(1)}, bf16[2,16,128]{2,1,0:T(8,128)(2,1)}, u32[]{:S(2)}) copy-start(bf16[2,16,128]{2,1,0:T(8,128)(2,1)} %fusion.46) | copy-start | bytes 24580
  117.2 5.0 %copy-start.14 = (bf16[128,128]{1,0:T(8,128)(2,1)S(1)}, bf16[128,128]{1,0:T(8,128)(2,1)}, u32[]{:S(2)}) copy-start(bf16[128,128]{1,0:T(8,128)(2,1)} %param.28) | copy-start | bytes 98308
  117.3 38.5 %copy-start.3 = (bf16[8,128,32]{1,0,2:T(8,128)(2,1)S(1)}, bf16[8,128,32]{1,0,2:T(8,128)(2,1)}, u32[]{:S(2)}) copy-start(bf16[8,128,32]{1,0,2:T(8,128)(2,1)} %copy.123) | copy-start | bytes 196612
  117.8 52.8 %copy-start.15 = (bf16[128,128]{1,0:T(8,128)(2,1)S(1)}, bf16[128,128]{1,0:T(8,128)(2,1)}, u32[]{:S(2)}) copy-start(bf16[128,128]{1,0:T(8,128)(2,1)} %param.29) | copy-start | bytes 98308
  118.7 56.0 %copy-start.1 = (bf16[32,8,256]{2,1,0:T(8,128)(2,1)S(1)}, bf16[32,8,256]{2,1,0:T(8,128)(2,1)}, u32[]{:S(2)}) copy-start(bf16[32,8,256]{2,1,0:T(8,128)(2,1)} %param.15) | copy-start | bytes 393220
  118.7 10.7 %all-to-all-start.1 = ((bf16[4,2,8192]{2,1,0:T(2,128)(2,1)}), bf16[4,2,8192]{2,1,0:T(2,128)(2,1)S(1)}, u32[]{:S(2)}, u32[]{:S(2)}) async-start(bf16[4,2,8192]{2,1,0:T(2,128)(2,1)} %reshape.243), calls=%async_computation.1 | async-start | bytes 262144 | tf_op jit(solution)/shard_map/all_to_all | solution.py:38
  156.8 12.1 %all-to-all-start.5 = ((f32[4,1,1024]{2,1,0:T(1,128)}), f32[4,1,1024]{2,1,0:T(1,128)S(1)}, u32[]{:S(2)}, u32[]{:S(2)}) async-start(f32[4,1,1024]{2,1,0:T(1,128)} %reshape.247), calls=%async_computation.5 | async-start | bytes 32768 | tf_op jit(solution)/shard_map/all_to_all | solution.py:179
  171.4 10.0 %all-to-all-start.6 = ((bf16[4,2,16,128]{3,2,1,0:T(8,128)(2,1)}), bf16[4,2,16,128]{3,2,1,0:T(8,128)(2,1)S(1)}, u32[]{:S(2)}, u32[]{:S(2)}) async-start(bf16[4,2,16,128]{3,2,1,0:T(8,128)(2,1)} %broadcast_in_dim.11), calls=%async_computation.6 | async-start | bytes 65536 | tf_op jit(solution)/shard_map/all_to_all | solution.py:17
Sparse Core Ops, SparseCore 0:
  26.6 44.8 all-gather.3
  102.3 51.9 all-gather.5
where the time goes:
time: 192 us; the launch traced here: 189 us
  waiting for transfers between devices  62.6 us (33%)
  starting transfers between devices  40.8 us (21%)
  local copies, waits for them, and re-layouts  32.9 us (17%)
  blocking collectives  23.6 us (12%)
  between operations  14.7 us (8%)
  other arithmetic  7.55 us (4%)
  matrix products  6.74 us (4%)
    all_to_all x4, starting transfers between devices, sent_to_all(): return lax.all_to_all(copies, axis, split_axis=0, concat_axis=0, tiled=True)  26.7 us
    all_gather x1, waiting for transfers between devices, from_root(): lax.all_gather(array, axis)  24.7 us
    all_gather x1, blocking collectives, side_by_side(): result = lax.all_gather(both, axis, axis=dim, tiled=True)  23.6 us
    all_to_all x4, waiting for transfers between devices, sent_to_all(): return lax.all_to_all(copies, axis, split_axis=0, concat_axis=0, tiled=True)  19.5 us
    unnamed x47, local copies, waits for them, and re-layouts  13.5 us
    all_to_all x2, waiting for transfers between devices, summed_on_arrival(): lax.all_to_all(in_blocks(array, dim, length), axis, 0, 0, tiled=True)  11.8 us
    all_to_all x2, starting transfers between devices, summed_on_arrival(): lax.all_to_all(in_blocks(array, dim, length), axis, 0, 0, tiled=True)  8.61 us
    all_to_all x1, waiting for transfers between devices, per_device(): lax.all_to_all(product, 'branch', split_axis=0, concat_axis=2, tiled=True)  6.57 us
  transfers between devices with their start and end apart: 9, of which 7 were waited for; matrix products, arithmetic and copies ran while one was open for 19% of the time, Pallas kernels for 0%

commit v1 on v0

v1 whole, which is shorter than its diff:
```python
import jax
import jax.numpy as jnp
from jax import lax
from jax.experimental import pallas as pl
from jax.experimental.pallas import tpu as pltpu
from jax.sharding import PartitionSpec as P

EPS = 1e-05
MESH = pl.DeviceIdType.MESH
BF = jnp.bfloat16
F32 = jnp.float32
NB, NR, NC = 4, 16, 8
HEADS, DEPTH = 2, 32


def standardise(x):
    centred = x - jnp.mean(x, axis=-1, keepdims=True)
    variance = jnp.mean(centred * centred, axis=-1, keepdims=True)
    return centred * lax.rsqrt(variance + EPS)


def mm(a, b):
    return jnp.dot(a, b, preferred_element_type=F32)


def mm_nt(a, b):
    return lax.dot_general(a, b, (((1,), (1,)), ((), ())), preferred_element_type=F32)


def mm_tn(a, b):
    return lax.dot_general(a, b, (((0,), (0,)), ((), ())), preferred_element_type=F32)


def iota(shape, dim):
    return lax.broadcasted_iota(jnp.int32, shape, dim)


def kernel(
    hom,
    coup,
    coup_t,
    w_att,
    w_lr,
    w_fin,
    w_off,
    w_prod,
    w_tri,
    w_close,
    w_change,
    msa_out,
    pair_out,
    l_send, lbuf, r_send, rbuf, xa, b_send, bb1, b2_send, bb2, tw, midbuf,
    tl_send, tlbuf, tr_scr, tr_send, trbuf, tlf, trf, obuf,
    ctx_send, cb, p_send, pbuf, att,
    s_l, s_r, s_x, s_b1, s_b2, s_w, s_mid, s_tl, s_tr, s_o, s_c, s_p,
):
    b = lax.axis_index("branch")
    r = lax.axis_index("row")
    c = lax.axis_index("col")
    active = (b // 2) == (r % 2)
    c_dest = r // 2
    r_src = 2 * c + b // 2
    same_col = c_dest == c

    barrier = pltpu.get_barrier_semaphore()

    def greet(axis, me, size):
        def body(d, _):
            pl.semaphore_signal(
                barrier, inc=1, device_id={axis: (me + d) % size}, device_id_type=MESH
            )
            return 0

        lax.fori_loop(1, size, body, 0)

    greet("row", r, NR)
    greet("col", c, NC)
    greet("branch", b, NB)

    def greet_source(k, _):
        @pl.when(jnp.logical_or(r_src != r, k != c))
        def _():
            pl.semaphore_signal(
                barrier, inc=1, device_id={"row": r_src, "col": k}, device_id_type=MESH
            )

        return 0

    lax.fori_loop(0, NC, greet_source, 0)

    normed = standardise(hom[...].astype(F32)).astype(BF)
    y = mm(normed, w_lr[...])
    row_i = iota((256, 256), 0) % 8
    lane = iota((256, 256), 1)
    pick = (iota((32, 256), 1) // 8 == iota((32, 256), 0)).astype(BF)
    left = jnp.where(lane % 8 == row_i, y[:, :256], 0.0).astype(BF)
    right = jnp.where(lane // 32 == row_i, y[:, 256:], 0.0).astype(BF)
    l_send[...] = mm(pick, left).astype(BF)
    right = mm(pick, right).astype(BF)
    r_send[...] = jnp.where(b % 2 == 0, right[:, :128], right[:, 128:])

    pair_normed = standardise(coup[...].astype(F32)).astype(BF)
    offs = w_off[...]
    off_row = iota((16, 128), 0) % 8
    tile = jnp.zeros((16, 16), F32)
    for i in range(8):
        tile = tile + mm_nt(
            jnp.where(off_row == i, offs, jnp.zeros_like(offs)), pair_normed[16 * i : 16 * i + 16]
        )
    place = (iota((16, 128), 1) == iota((16, 128), 0) + 16 * c).astype(BF)
    b_send[...] = mm(tile.astype(BF), place).astype(BF)

    pl.semaphore_wait(barrier, 25 + jnp.where(active, jnp.where(same_col, 15, 16), 0))

    def send_group(axis, me, size, source, dest, sems):
        def body(d, _):
            peer = (me + d) % size
            pltpu.make_async_remote_copy(
                src_ref=source(peer),
                dst_ref=dest.at[me],
                send_sem=sems.at[0],
                recv_sem=sems.at[1],
                device_id={axis: peer},
                device_id_type=MESH,
            ).start()
            return 0

        lax.fori_loop(1, size, body, 0)

    def send_right(source, dest, sems):
        @pl.when(active)
        def _():
            def body(peer, _):
                @pl.when(jnp.logical_or(peer != r, jnp.logical_not(same_col)))
                def _():
                    pltpu.make_async_remote_copy(
                        src_ref=source,
                        dst_ref=dest.at[c],
                        send_sem=sems.at[0],
                        recv_sem=sems.at[1],
                        device_id={"row": peer, "col": c_dest},
                        device_id_type=MESH,
                    ).start()

                return 0

            lax.fori_loop(0, NR, body, 0)

            @pl.when(same_col)
            def _():
                pltpu.make_async_copy(source, dest.at[c], sems.at[1]).start()

    def wait_bytes(ref, sem):
        pltpu.make_async_copy(ref, ref, sem).wait()

    def arrived(dest, size, sems):
        wait_bytes(dest.at[pl.ds(0, size)], sems.at[1])

    def left_device(dest, size, sems):
        wait_bytes(dest.at[pl.ds(0, size)], sems.at[0])

    def left_right(dest, sems):
        @pl.when(active)
        def _():
            def body(peer, _):
                @pl.when(jnp.logical_or(peer != r, jnp.logical_not(same_col)))
                def _():
                    wait_bytes(dest.at[0], sems.at[0])

                return 0

            lax.fori_loop(0, NR, body, 0)

    send_group("col", c, NC, lambda peer: l_send, lbuf, s_l)
    send_right(r_send, rbuf, s_r)
    send_group("col", c, NC, lambda peer: b_send, bb1, s_b1)
    send_group("row", r, NR, lambda peer: hom.at[pl.ds(16 * peer, 16)], xa, s_x)
    send_group("branch", b, NB, lambda peer: w_tri, tw, s_w)
    lbuf[c] = l_send[...]
    bb1[c] = b_send[...]
    xa[r] = hom[pl.ds(pl.multiple_of(16 * r, 16), 16), :]
    tw[b] = w_tri[...]

    arrived(bb1, NC - 1, s_b1)
    b2_send[...] = jnp.sum(bb1[...].astype(F32), axis=0).astype(BF)
    send_group("row", r, NR, lambda peer: b2_send, bb2, s_b2)
    bb2[r] = b2_send[...]

    arrived(lbuf, NC - 1, s_l)
    arrived(rbuf, NC, s_r)
    outer = mm_tn(lbuf[...].reshape(256, 256), rbuf[...].reshape(256, 128))
    turned = [outer] + [pltpu.roll(outer, 32 * k, 1) for k in range(1, 4)]
    turned = [t.reshape(8, 4, 8, 128) for t in turned]
    block = iota((8, 8, 128), 2) // 32
    rows = []
    for j in range(4):
        x = jnp.zeros((8, 8, 128), F32)
        for u in range(4):
            x = jnp.where(block == u, turned[(u - j) % 4][:, u], x)
        rows.append(jnp.concatenate([x[t] for t in range(8)], axis=1))
    x = jnp.concatenate(rows, axis=0).astype(BF)
    update = mm(x, w_prod[...]) * (1.0 / 256.0)
    mid = (coup_t[b].astype(F32) + update).astype(BF)
    midbuf[b] = mid
    send_group("branch", b, NB, lambda peer: midbuf.at[b], midbuf, s_mid)
    own_normed = standardise(mid.astype(F32)).astype(BF)
    closing = jax.nn.sigmoid(mm(own_normed, w_close[...]))

    arrived(xa, NR - 1, s_x)
    att[...] = mm(standardise(xa[...].astype(F32).reshape(256, 256)).astype(BF), w_att[...])

    arrived(tw, NB - 1, s_w)
    arrived(midbuf, NB - 1, s_mid)
    tri = standardise(midbuf[...].astype(F32).reshape(128, 128)).astype(BF)

    def tri_linear(kind):
        return mm_nt(tri, tw[:, kind].reshape(128, 128))

    tl_send[...] = (jax.nn.sigmoid(tri_linear(1)) * tri_linear(0)).astype(BF)
    send_group("col", c, NC, lambda peer: tl_send, tlbuf, s_tl)
    tr_scr[...] = jax.nn.sigmoid(tri_linear(3)) * tri_linear(2)
    for jj in range(4):
        tr_send[16 * jj : 16 * jj + 16, :] = tr_scr[
            pl.ds(4 * (b % 2) + jj, 16, stride=8), :
        ].astype(BF)
    send_right(tr_send, trbuf, s_tr)
    tlbuf[c] = tl_send[...]

    arrived(bb2, NR - 1, s_b2)
    bias = bb2[...].astype(F32)
    y4 = att[...].reshape(16, 2, 8, 512)
    head_lane = iota((128, 128), 1) // DEPTH
    contexts = []
    for s in range(2):
        ys = y4[:, s].reshape(128, 512)
        q = ys[:, :128].astype(BF)
        k = ys[:, 128:256].astype(BF)
        v = ys[:, 256:384].astype(BF)
        context = jnp.zeros((128, 128), F32)
        for h in range(HEADS):
            qh = jnp.where(head_lane == h, q, jnp.zeros_like(q))
            scores = mm_nt(qh, k) * (float(DEPTH) ** -0.5)
            scores = scores + bias[:, 8 * h : 8 * h + 8].reshape(128, 128)
            expo = jnp.exp(scores - jnp.max(scores, axis=-1, keepdims=True))
            total = jnp.sum(expo, axis=-1, keepdims=True)
            context = jnp.where(head_lane == h, mm(expo.astype(BF), v) / total, context)
        context = context * jax.nn.sigmoid(ys[:, 384:])
        contexts.append(context.reshape(16, 8, 128))
    ctx_send[...] = jnp.concatenate(contexts, axis=1).astype(BF)
    send_group("row", r, NR, lambda peer: ctx_send.at[peer], cb, s_c)
    cb[r] = ctx_send[r]

    arrived(tlbuf, NC - 1, s_tl)
    arrived(trbuf, NC, s_tr)
    tlf[...] = tlbuf[...].astype(F32)
    trf[...] = trbuf[...].astype(F32)

    def product_step(k, acc):
        acc = list(acc)
        for kk in range(16):
            t = tlf[k, 8 * kk : 8 * kk + 8, :]
            for j in range(4):
                acc[j] = acc[j] + t * trf[k, 16 * j + kk : 16 * j + kk + 1, :]
        return tuple(acc)

    product = lax.fori_loop(
        0, NC, product_step, tuple(jnp.zeros((8, 128), F32) for _ in range(4))
    )
    product_normed = standardise(jnp.concatenate(product, axis=0)).astype(BF)
    change = mm(product_normed, w_change[...])
    obuf[b] = (mid.astype(F32) + closing * change).astype(BF)
    send_group("branch", b, NB, lambda peer: obuf.at[b], obuf, s_o)

    arrived(cb, NR - 1, s_c)
    ctx = cb[...].astype(F32).reshape(256, 128).astype(BF)
    half = iota((16, 8, 128), 2) < 64
    for n in range(NB):
        part = mm(ctx, w_fin[n]).reshape(16, 2, 8, 128)
        p_send[n] = jnp.where(half, part[:, 0], part[:, 1]).reshape(128, 128).astype(BF)
    send_group("branch", b, NB, lambda peer: p_send.at[peer], pbuf, s_p)
    pbuf[b] = p_send[b]
    choose = (iota((256, 128), 0) == 64 * b + iota((256, 128), 1) % 64).astype(BF)
    own = mm(hom[...], choose).reshape(16, 2, 8, 128)
    own = jnp.where(half, own[:, 0], own[:, 1]).reshape(128, 128)

    arrived(obuf, NB - 1, s_o)
    pair_out[...] = obuf[...]
    arrived(pbuf, NB - 1, s_p)
    msa_out[...] = (own + jnp.sum(pbuf[...].astype(F32), axis=0)).astype(BF)

    left_device(lbuf, NC - 1, s_l)
    left_right(rbuf, s_r)
    left_device(bb1, NC - 1, s_b1)
    left_device(xa, NR - 1, s_x)
    left_device(tw, NB - 1, s_w)
    left_device(bb2, NR - 1, s_b2)
    left_device(midbuf, NB - 1, s_mid)
    left_device(tlbuf, NC - 1, s_tl)
    left_right(trbuf, s_tr)
    left_device(cb, NR - 1, s_c)
    left_device(obuf, NB - 1, s_o)
    left_device(pbuf, NB - 1, s_p)


def per_device(
    homolog_tensor,
    couple_tensor,
    probe_matrix,
    lookup_matrix,
    content_matrix,
    scoring_sigmoid_matrix,
    scoring_final_matrix,
    couple_offset_matrix,
    product_first_matrix,
    product_second_matrix,
    product_final_matrix,
    trio_first_matrix,
    trio_second_matrix,
    trio_sigmoid_matrix,
    trio_final_matrix,
):
    hom = homolog_tensor.reshape(256, 256)
    coup = couple_tensor.reshape(128, 128)
    coup_t = jnp.transpose(couple_tensor, (1, 0, 2)).reshape(4, 32, 128)
    w_att = jnp.concatenate(
        [
            jnp.pad(w, ((0, 0), (0, 64)))
            for w in (probe_matrix, lookup_matrix, content_matrix, scoring_sigmoid_matrix)
        ],
        axis=1,
    )
    w_lr = jnp.concatenate(
        [jnp.repeat(product_first_matrix, 8, axis=1), jnp.tile(product_second_matrix, (1, 8))],
        axis=1,
    )
    w_fin = jnp.transpose(scoring_final_matrix.reshape(64, 4, 64), (1, 0, 2))
    w_fin = jnp.pad(jnp.concatenate([w_fin, w_fin], axis=2), ((0, 0), (0, 64), (0, 0)))
    w_off = jnp.repeat(couple_offset_matrix.T, 8, axis=0)
    w_tri = jnp.transpose(jnp.concatenate([trio_first_matrix, trio_second_matrix]), (0, 2, 1))
    vmem = pl.BlockSpec(memory_space=pltpu.VMEM)
    scratch = [
        ((32, 256), BF),
        ((8, 32, 256), BF),
        ((32, 128), BF),
        ((8, 32, 128), BF),
        ((16, 16, 256), BF),
        ((16, 128), BF),
        ((8, 16, 128), BF),
        ((16, 128), BF),
        ((16, 16, 128), BF),
        ((4, 4, 32, 128), BF),
        ((4, 32, 128), BF),
        ((128, 128), BF),
        ((8, 128, 128), BF),
        ((128, 128), F32),
        ((64, 128), BF),
        ((8, 64, 128), BF),
        ((8, 128, 128), F32),
        ((8, 64, 128), F32),
        ((4, 32, 128), BF),
        ((16, 16, 128), BF),
        ((16, 16, 128), BF),
        ((4, 128, 128), BF),
        ((4, 128, 128), BF),
        ((256, 512), F32),
    ]
    msa, pair = pl.pallas_call(
        kernel,
        out_shape=(
            jax.ShapeDtypeStruct((128, 128), BF),
            jax.ShapeDtypeStruct((4, 32, 128), BF),
        ),
        in_specs=[vmem] * 11,
        out_specs=(vmem, vmem),
        scratch_shapes=[pltpu.VMEM(*s) for s in scratch] + [pltpu.SemaphoreType.DMA((2,))] * 12,
        compiler_params=pltpu.CompilerParams(
            collective_id=0, has_side_effects=True, vmem_limit_bytes=32 * 1024 * 1024
        ),
        name="block",
    )(
        hom,
        coup,
        coup_t,
        w_att,
        w_lr,
        w_fin,
        w_off,
        product_final_matrix,
        w_tri,
        trio_sigmoid_matrix,
        trio_final_matrix,
    )
    revised = jnp.transpose(msa.reshape(16, 8, 2, 64), (0, 2, 1, 3)).reshape(32, 8, 64)
    pairwise = jnp.transpose(pair.reshape(16, 8, 128), (1, 0, 2))
    return (revised, pairwise)


def solution(mesh):
    return jax.shard_map(
        per_device,
        mesh=mesh,
        in_specs=(
            P("col", "row", None),
            P("row", "col", None),
            P(None, "branch"),
            P(None, "branch"),
            P(None, "branch"),
            P(None, "branch"),
            P("branch", None),
            P(None, "branch"),
            P(),
            P(),
            P(),
            P(None, None, "branch"),
            P(None, None, "branch"),
            P(),
            P(),
        ),
        out_specs=(P("col", "row", "branch"), P("row", "col", None)),
        check_vma=False,
    )
```

time: 192 us -> 53.5 us (0.28); the launches traced: 189 us -> 52.8 us
  waiting for transfers between devices: 62.6 us -> 0 us
  Pallas kernels: 0 us -> 43.1 us
  starting transfers between devices: 40.8 us -> 0 us
  local copies, waits for them, and re-layouts: 32.9 us -> 8.85 us
  blocking collectives: 23.6 us -> 0 us
  between operations: 14.7 us -> 0.78 us
  other arithmetic: 7.55 us -> 0.15 us
  matrix products: 6.74 us -> 0 us
    pallas_call x0 -> x1, Pallas kernels: none -> 43.1 us  [per_device(): pl.pallas_call(kernel, out_shape=(jax.ShapeDtypeStruct((128, 128), BF), j...]
    all_to_all x7 -> x0, starting transfers between devices: 40.7 us -> none  [the longest x4 26.7 us: sent_to_all(): return lax.all_to_all(copies, axis, split_axis=0, concat_axis=0, tiled=True)]
    all_to_all x7 -> x0, waiting for transfers between devices: 37.9 us -> none  [the longest x4 19.5 us: sent_to_all(): return lax.all_to_all(copies, axis, split_axis=0, concat_axis=0, tiled=True)]
    all_gather x2 -> x0, waiting for transfers between devices: 24.7 us -> none  [the longest x1 24.7 us: from_root(): lax.all_gather(array, axis)]
    all_gather x1 -> x0, blocking collectives: 23.6 us -> none  [side_by_side(): result = lax.all_gather(both, axis, axis=dim, tiled=True)]
    dot_general x19 -> x0, matrix products: 6.74 us -> none  [the longest x14 3.6 us: apply_linear(): jnp.dot(source.reshape(-1, weights.shape[0]), weights, preferred_element_...]
    unnamed x47 -> x34, local copies, waits for them, and re-layouts: 13.5 us -> 7.16 us
    split x2 -> x0, local copies, waits for them, and re-layouts: 5.36 us -> none  [side_by_side(): jnp.split(result, [sum(widths[:k]) for k in range(1, len(widths))], axis=...]
  transfers between devices with their start and end apart: 9 -> 0, of which waited for: 7 -> 0; matrix products, arithmetic and copies ran while one was open for 19% -> 0% of each run, Pallas kernels for 0% -> 0%
where the time goes in v1:
time: 53.5 us; the launch traced here: 52.8 us
  Pallas kernels  43.1 us (81%)
  local copies, waits for them, and re-layouts  8.85 us (17%)
  between operations  0.78 us (1%)
    pallas_call x1, Pallas kernels, per_device(): pl.pallas_call(kernel, out_shape=(jax.ShapeDtypeStruct((128, 128), BF), j...  43.1 us
    unnamed x34, local copies, waits for them, and re-layouts  7.16 us

profile of v1, /device:TPU:1, one launch (start us, length us, event | category | flops | bytes accessed | tf_op | source)
XLA Modules:
  0.0 52.8 jit_solution(13398873538869677292)
XLA Ops:
  0.6 0.0 copy-start
  0.6 0.7 %copy-done = bf16[256,32]{0,1:T(8,128)(2,1)S(1)} copy-done((bf16[256,32]{0,1:T(8,128)(2,1)S(1)}, bf16[256,32]{0,1:T(8,128)(2,1)}, u32[]{:S(2)}) %copy-start) | copy-done | bytes 16408
  1.4 0.0 copy-start.11
  1.4 0.1 copy.31
  1.5 0.6 %copy-done.11 = bf16[256,32]{0,1:T(8,128)(2,1)S(1)} copy-done((bf16[256,32]{0,1:T(8,128)(2,1)S(1)}, bf16[256,32]{0,1:T(8,128)(2,1)}, u32[]{:S(2)}) %copy-start.11) | copy-done | bytes 16408
  2.1 0.0 copy-start.6
  2.1 0.1 copy.32
  2.2 0.6 %copy-done.6 = bf16[256,64]{0,1:T(8,128)(2,1)S(1)} copy-done((bf16[256,64]{0,1:T(8,128)(2,1)S(1)}, bf16[256,64]{0,1:T(8,128)(2,1)}, u32[]{:S(2)}) %copy-start.6) | copy-done | bytes 32792
  2.9 0.0 copy-start.7
  2.9 0.1 copy.27
  3.0 0.6 %copy-done.7 = bf16[256,64]{0,1:T(8,128)(2,1)S(1)} copy-done((bf16[256,64]{0,1:T(8,128)(2,1)S(1)}, bf16[256,64]{0,1:T(8,128)(2,1)}, u32[]{:S(2)}) %copy-start.7) | copy-done | bytes 32792
  3.6 0.0 copy-start.8
  3.6 0.1 copy.28
  3.7 0.6 %copy-done.8 = bf16[256,64]{0,1:T(8,128)(2,1)S(1)} copy-done((bf16[256,64]{0,1:T(8,128)(2,1)S(1)}, bf16[256,64]{0,1:T(8,128)(2,1)}, u32[]{:S(2)}) %copy-start.8) | copy-done | bytes 32792
  4.4 0.0 copy-start.9
  4.4 0.1 copy.29
  4.5 0.6 %copy-done.9 = bf16[256,64]{0,1:T(8,128)(2,1)S(1)} copy-done((bf16[256,64]{0,1:T(8,128)(2,1)S(1)}, bf16[256,64]{0,1:T(8,128)(2,1)}, u32[]{:S(2)}) %copy-start.9) | copy-done | bytes 32792
  5.1 0.1 copy.30
  5.3 0.0 copy-start.10
  5.3 0.1 fusion.7
  5.3 0.7 %copy-done.10 = bf16[64,256]{1,0:T(8,128)(2,1)S(1)} copy-done((bf16[64,256]{1,0:T(8,128)(2,1)S(1)}, bf16[64,256]{1,0:T(8,128)(2,1)}, u32[]{:S(2)}) %copy-start.10) | copy-done | bytes 32792
  6.0 0.0 copy-start.1
  6.0 0.1 reshape.39
  6.1 0.0 copy-start.3
  6.2 0.0 copy-start.2
  6.2 0.1 fusion.11.w_fin
  6.3 0.6 %copy-done.3 = bf16[8,16,128]{2,1,0:T(8,128)(2,1)S(1)} copy-done((bf16[8,16,128]{2,1,0:T(8,128)(2,1)S(1)}, bf16[8,16,128]{2,1,0:T(8,128)(2,1)}, u32[]{:S(2)}) %copy-start.3) | copy-done | bytes 32792
  6.9 0.0 copy-start.12
  6.9 0.0 copy-start.13
  6.9 0.7 %copy-done.12 = bf16[2,128,32]{1,2,0:T(8,128)(2,1)S(1)} copy-done((bf16[2,128,32]{1,2,0:T(8,128)(2,1)S(1)}, bf16[2,128,32]{1,2,0:T(8,128)(2,1)}, u32[]{:S(2)}) %copy-start.12) | copy-done | bytes 16408
  7.6 0.0 copy-done.13
  7.6 0.0 copy-start.4
  7.6 0.0 copy-start.5
  7.7 0.0 copy-start.14
  7.7 0.7 %copy-done.14 = bf16[128,2]{0,1:T(2,128)(2,1)S(1)} copy-done((bf16[128,2]{0,1:T(2,128)(2,1)S(1)}, bf16[128,2]{0,1:T(2,128)(2,1)}, u32[]{:S(2)}) %copy-start.14) | copy-done | bytes 536
  8.3 0.0 copy-done.1
  8.3 0.0 copy-done.2
  8.3 0.1 copy-done.4
  8.4 0.0 copy-done.5
  8.4 43.1 %block.1 = (bf16[128,128]{1,0:T(8,128)(2,1)S(1)}, bf16[4,32,128]{2,1,0:T(8,128)(2,1)S(1)}) custom-call(bf16[256,256]{1,0:T(8,128)(2,1)S(1)} %bitcast.21, bf16[128,128]{1,0:T(8,128)(2,1)S(1)} %bitcast.23, bf16[4,32,128]{2,1,0:T(8,128)(2,1)S(1)} %bitcast.24, bf16[256,512]{1,0:T(8,128)(2,1)S(1)} %get-tuple-element.6.w_att, ...), custom_call_target="tpu_custom_call" | custom-call | tf_op jit(solution)/shard_map/block/pallas_call | solution.py:367
  51.5 0.1 reshape.41
  51.6 0.6 %copy.34 = bf16[16,2,8,64]{3,2,1,0:T(8,128)(2,1)} copy(bf16[16,2,8,64]{3,1,2,0:T(2,128)(2,1)S(1)} %bitcast.28) | data formatting | bytes 65536 | tf_op jit(solution)/shard_map/transpose | solution.py:393
  52.2 0.6 %copy.39 = bf16[16,8,128]{2,0,1:T(8,128)(2,1)} copy(bf16[16,8,128]{2,1,0:T(8,128)(2,1)S(1)} %bitcast.25) | data formatting | bytes 65536 | tf_op jit(solution)/shard_map/reshape | solution.py:394
  (6 shorter events, 0.1 us)
Async XLA Ops:
  0.6 0.7 %copy-start = (bf16[256,32]{0,1:T(8,128)(2,1)S(1)}, bf16[256,32]{0,1:T(8,128)(2,1)}, u32[]{:S(2)}) copy-start(bf16[256,32]{0,1:T(8,128)(2,1)} %param.23) | copy-start | bytes 49156
  1.4 0.7 %copy-start.11 = (bf16[256,32]{0,1:T(8,128)(2,1)S(1)}, bf16[256,32]{0,1:T(8,128)(2,1)}, u32[]{:S(2)}) copy-start(bf16[256,32]{0,1:T(8,128)(2,1)} %param.24) | copy-start | bytes 49156
  2.1 0.8 %copy-start.6 = (bf16[256,64]{0,1:T(8,128)(2,1)S(1)}, bf16[256,64]{0,1:T(8,128)(2,1)}, u32[]{:S(2)}) copy-start(bf16[256,64]{0,1:T(8,128)(2,1)} %param.17) | copy-start | bytes 98308
  2.9 0.8 %copy-start.7 = (bf16[256,64]{0,1:T(8,128)(2,1)S(1)}, bf16[256,64]{0,1:T(8,128)(2,1)}, u32[]{:S(2)}) copy-start(bf16[256,64]{0,1:T(8,128)(2,1)} %param.18) | copy-start | bytes 98308
  3.6 0.8 %copy-start.8 = (bf16[256,64]{0,1:T(8,128)(2,1)S(1)}, bf16[256,64]{0,1:T(8,128)(2,1)}, u32[]{:S(2)}) copy-start(bf16[256,64]{0,1:T(8,128)(2,1)} %param.19) | copy-start | bytes 98308
  4.4 0.8 %copy-start.9 = (bf16[256,64]{0,1:T(8,128)(2,1)S(1)}, bf16[256,64]{0,1:T(8,128)(2,1)}, u32[]{:S(2)}) copy-start(bf16[256,64]{0,1:T(8,128)(2,1)} %param.20) | copy-start | bytes 98308
  5.3 0.8 %copy-start.10 = (bf16[64,256]{1,0:T(8,128)(2,1)S(1)}, bf16[64,256]{1,0:T(8,128)(2,1)}, u32[]{:S(2)}) copy-start(bf16[64,256]{1,0:T(8,128)(2,1)} %param.21) | copy-start | bytes 98308
  6.0 2.3 %copy-start.1 = (bf16[1024,128]{1,0:T(8,128)(2,1)S(1)}, bf16[1024,128]{1,0:T(8,128)(2,1)}, u32[]{:S(2)}) copy-start(bf16[1024,128]{1,0:T(8,128)(2,1)} %w_prod.1) | copy-start | bytes 786436
  6.1 0.8 %copy-start.3 = (bf16[8,16,128]{2,1,0:T(8,128)(2,1)S(1)}, bf16[8,16,128]{2,1,0:T(8,128)(2,1)}, u32[]{:S(2)}) copy-start(bf16[8,16,128]{2,1,0:T(8,128)(2,1)} %param.16) | copy-start | bytes 98308
  6.2 2.2 %copy-start.2 = (bf16[32,8,256]{2,1,0:T(8,128)(2,1)S(1)}, bf16[32,8,256]{2,1,0:T(8,128)(2,1)}, u32[]{:S(2)}) copy-start(bf16[32,8,256]{2,1,0:T(8,128)(2,1)} %param.15) | copy-start | bytes 393220
  6.9 0.7 %copy-start.12 = (bf16[2,128,32]{1,2,0:T(8,128)(2,1)S(1)}, bf16[2,128,32]{1,2,0:T(8,128)(2,1)}, u32[]{:S(2)}) copy-start(bf16[2,128,32]{1,2,0:T(8,128)(2,1)} %param.27) | copy-start | bytes 49156
  6.9 0.7 %copy-start.13 = (bf16[2,128,32]{1,2,0:T(8,128)(2,1)S(1)}, bf16[2,128,32]{1,2,0:T(8,128)(2,1)}, u32[]{:S(2)}) copy-start(bf16[2,128,32]{1,2,0:T(8,128)(2,1)} %param.26) | copy-start | bytes 49156
  7.6 0.8 %copy-start.4 = (bf16[128,128]{1,0:T(8,128)(2,1)S(1)}, bf16[128,128]{1,0:T(8,128)(2,1)}, u32[]{:S(2)}) copy-start(bf16[128,128]{1,0:T(8,128)(2,1)} %w_close.1) | copy-start | bytes 98308
  7.6 0.8 %copy-start.5 = (bf16[128,128]{1,0:T(8,128)(2,1)S(1)}, bf16[128,128]{1,0:T(8,128)(2,1)}, u32[]{:S(2)}) copy-start(bf16[128,128]{1,0:T(8,128)(2,1)} %w_change.1) | copy-start | bytes 98308
  7.7 0.7 %copy-start.14 = (bf16[128,2]{0,1:T(2,128)(2,1)S(1)}, bf16[128,2]{0,1:T(2,128)(2,1)}, u32[]{:S(2)}) copy-start(bf16[128,2]{0,1:T(2,128)(2,1)} %param.22) | copy-start | bytes 1540

commit v2 on v1

v2 whole, which is shorter than its diff:
```python
import jax
import jax.numpy as jnp
from jax import lax
from jax.experimental import pallas as pl
from jax.experimental.pallas import tpu as pltpu
from jax.sharding import PartitionSpec as P

EPS = 1e-05
MESH = pl.DeviceIdType.MESH
BF = jnp.bfloat16
F32 = jnp.float32
NB, NR, NC = 4, 16, 8
HEADS, DEPTH = 2, 32


def standardise(x):
    centred = x - jnp.mean(x, axis=-1, keepdims=True)
    variance = jnp.mean(centred * centred, axis=-1, keepdims=True)
    return centred * lax.rsqrt(variance + EPS)


def mm(a, b):
    return jnp.dot(a, b, preferred_element_type=F32)


def mm_nt(a, b):
    return lax.dot_general(a, b, (((1,), (1,)), ((), ())), preferred_element_type=F32)


def mm_tn(a, b):
    return lax.dot_general(a, b, (((0,), (0,)), ((), ())), preferred_element_type=F32)


def iota(shape, dim):
    return lax.broadcasted_iota(jnp.int32, shape, dim)


def kernel(
    hom_hbm,
    coup_hbm,
    wq_hbm, wk_hbm, wv_hbm, wg_hbm,
    wf_hbm,
    wo_hbm,
    wl_hbm, wr_hbm,
    prod_hbm,
    t1_hbm, t2_hbm,
    close_hbm, change_hbm,
    msa_out,
    pair_out,
    hom, coup, wq, wk, wv, wg, wf, wo, wl, wr, w_prod, w_close, w_change,
    l_send, lbuf, r_send, rbuf, xa, b_send, bb1, b2_send, bb2, tw, midbuf, coup_f,
    tl_send, tlbuf, tr_scr, tr_send, trbuf, tlf, trf, obuf,
    ctx_send, cb, p_send, pbuf, aq, ak, av, ag,
    s_in, s_l, s_r, s_x, s_b1, s_b2, s_w, s_mid, s_tl, s_tr, s_o, s_c, s_p,
):
    b = lax.axis_index("branch")
    r = lax.axis_index("row")
    c = lax.axis_index("col")
    active = (b // 2) == (r % 2)
    c_dest = r // 2
    r_src = 2 * c + b // 2
    same_col = c_dest == c

    loads = {
        name: pltpu.make_async_copy(source, dest, s_in.at[n])
        for n, (name, source, dest) in enumerate(
            (
                ("hom", hom_hbm, hom),
                ("wl", wl_hbm, wl),
                ("wr", wr_hbm, wr),
                ("coup", coup_hbm, coup),
                ("wo", wo_hbm, wo),
                ("t1", t1_hbm, tw.at[b, pl.ds(0, 2)]),
                ("t2", t2_hbm, tw.at[b, pl.ds(2, 2)]),
                ("prod", prod_hbm, w_prod),
                ("wq", wq_hbm, wq),
                ("wk", wk_hbm, wk),
                ("wv", wv_hbm, wv),
                ("wg", wg_hbm, wg),
                ("close", close_hbm, w_close),
                ("change", change_hbm, w_change),
                ("wf", wf_hbm, wf),
            )
        )
    }
    for name in loads:
        loads[name].start()

    barrier = pltpu.get_barrier_semaphore()

    def wrapped(value, size):
        return jnp.where(value >= size, value - size, value)

    def greet(axis, me, size):
        def body(d, _):
            pl.semaphore_signal(
                barrier, inc=1, device_id={axis: wrapped(me + d, size)}, device_id_type=MESH
            )
            return 0

        lax.fori_loop(1, size, body, 0)

    greet("row", r, NR)
    greet("col", c, NC)
    greet("branch", b, NB)

    def greet_source(k, _):
        @pl.when(jnp.logical_or(r_src != r, k != c))
        def _():
            pl.semaphore_signal(
                barrier, inc=1, device_id={"row": r_src, "col": k}, device_id_type=MESH
            )

        return 0

    lax.fori_loop(0, NC, greet_source, 0)

    loads["wl"].wait()
    loads["wr"].wait()
    spread = (iota((256, 32), 0) // 8 == iota((256, 32), 1)).astype(BF)
    wl_wide = mm(spread, wl[...]).astype(BF)
    wr_wide = jnp.concatenate([wr[...]] * 8, axis=0)
    row_i = iota((256, 256), 0) % 8
    lane = iota((256, 256), 1)
    pick = (iota((32, 256), 1) // 8 == iota((32, 256), 0)).astype(BF)
    loads["hom"].wait()
    normed = standardise(hom[...].astype(F32)).astype(BF)
    left = jnp.where(lane % 8 == row_i, mm_nt(normed, wl_wide), 0.0).astype(BF)
    right = jnp.where(lane // 32 == row_i, mm_nt(normed, wr_wide), 0.0).astype(BF)
    l_send[...] = mm(pick, left).astype(BF)
    right = mm(pick, right).astype(BF)
    r_send[...] = jnp.where(b % 2 == 0, right[:, :128], right[:, 128:])

    pl.semaphore_wait(barrier, 25 + jnp.where(active, jnp.where(same_col, 15, 16), 0))

    def send_group(axis, me, size, source, dest, sems):
        def body(d, _):
            peer = wrapped(me + d, size)
            pltpu.make_async_remote_copy(
                src_ref=source(peer),
                dst_ref=dest.at[me],
                send_sem=sems.at[0],
                recv_sem=sems.at[1],
                device_id={axis: peer},
                device_id_type=MESH,
            ).start()
            return 0

        lax.fori_loop(1, size, body, 0)

    def send_right(source, dest, sems):
        @pl.when(active)
        def _():
            def body(peer, _):
                @pl.when(jnp.logical_or(peer != r, jnp.logical_not(same_col)))
                def _():
                    pltpu.make_async_remote_copy(
                        src_ref=source,
                        dst_ref=dest.at[c],
                        send_sem=sems.at[0],
                        recv_sem=sems.at[1],
                        device_id={"row": peer, "col": c_dest},
                        device_id_type=MESH,
                    ).start()

                return 0

            lax.fori_loop(0, NR, body, 0)

            @pl.when(same_col)
            def _():
                pltpu.make_async_copy(source, dest.at[c], sems.at[1]).start()

    def wait_bytes(ref, sem):
        pltpu.make_async_copy(ref, ref, sem).wait()

    def arrived(dest, size, sems):
        wait_bytes(dest.at[pl.ds(0, size)], sems.at[1])

    def left_device(dest, size, sems):
        wait_bytes(dest.at[pl.ds(0, size)], sems.at[0])

    def left_right(dest, sems):
        @pl.when(active)
        def _():
            def body(peer, _):
                @pl.when(jnp.logical_or(peer != r, jnp.logical_not(same_col)))
                def _():
                    wait_bytes(dest.at[0], sems.at[0])

                return 0

            lax.fori_loop(0, NR, body, 0)

    send_right(r_send, rbuf, s_r)
    send_group("col", c, NC, lambda peer: l_send, lbuf, s_l)
    lbuf[c] = l_send[...]

    loads["coup"].wait()
    loads["wo"].wait()
    coup_f[...] = coup[...].astype(F32)
    pair_normed = standardise(coup_f[...]).astype(BF)
    heads = wo[...].astype(F32)
    offs = jnp.concatenate(
        [jnp.broadcast_to(heads[h : h + 1], (8, 128)) for h in range(HEADS)], axis=0
    ).astype(BF)
    off_row = iota((16, 128), 0) % 8
    tile = jnp.zeros((16, 16), F32)
    for i in range(8):
        tile = tile + mm_nt(
            jnp.where(off_row == i, offs, jnp.zeros_like(offs)), pair_normed[16 * i : 16 * i + 16]
        )
    place = (iota((16, 128), 1) == iota((16, 128), 0) + 16 * c).astype(BF)
    b_send[...] = mm(tile.astype(BF), place).astype(BF)
    send_group("col", c, NC, lambda peer: b_send, bb1, s_b1)
    bb1[c] = b_send[...]
    send_group("row", r, NR, lambda peer: hom.at[pl.ds(16 * peer, 16)], xa, s_x)
    xa[r] = hom[pl.ds(pl.multiple_of(16 * r, 16), 16), :]
    loads["t1"].wait()
    loads["t2"].wait()
    send_group("branch", b, NB, lambda peer: tw.at[b], tw, s_w)
    coup_own = jnp.concatenate(
        [coup_f[pl.ds(4 * b + j, 8, stride=16), :] for j in range(4)], axis=0
    )

    loads["prod"].wait()
    arrived(lbuf, NC - 1, s_l)
    arrived(rbuf, NC, s_r)
    outer = mm_tn(lbuf[...].reshape(256, 256), rbuf[...].reshape(256, 128))
    turned = [outer] + [pltpu.roll(outer, 32 * k, 1) for k in range(1, 4)]
    turned = [t.reshape(8, 4, 8, 128) for t in turned]
    block = iota((8, 8, 128), 2) // 32
    rows = []
    for j in range(4):
        x = jnp.zeros((8, 8, 128), F32)
        for u in range(4):
            x = jnp.where(block == u, turned[(u - j) % 4][:, u], x)
        rows.append(jnp.concatenate([x[t] for t in range(8)], axis=1))
    x = jnp.concatenate(rows, axis=0).astype(BF)
    update = mm(x, w_prod[...]) * (1.0 / 256.0)
    mid = (coup_own + update).astype(BF)
    midbuf[b] = mid
    send_group("branch", b, NB, lambda peer: midbuf.at[b], midbuf, s_mid)

    arrived(bb1, NC - 1, s_b1)
    b2_send[...] = jnp.sum(bb1[...].astype(F32), axis=0).astype(BF)
    send_group("row", r, NR, lambda peer: b2_send, bb2, s_b2)
    bb2[r] = b2_send[...]

    for name in ("wq", "wk", "wv", "wg"):
        loads[name].wait()
    arrived(xa, NR - 1, s_x)
    att_normed = standardise(xa[...].astype(F32).reshape(256, 256)).astype(BF)

    def by_row(weights, dest):
        y = mm_nt(att_normed, weights).reshape(16, 2, 8, -1)
        for s in range(2):
            dest[s] = y[:, s].reshape(128, -1).astype(dest.dtype)

    by_row(wq[...], aq)
    by_row(wk[...], ak)
    by_row(jnp.concatenate([wv[...]] * 2, axis=0), av)
    by_row(jnp.concatenate([wg[...]] * 2, axis=0), ag)

    arrived(tw, NB - 1, s_w)
    arrived(midbuf, NB - 1, s_mid)
    tri = standardise(midbuf[...].astype(F32).reshape(128, 128)).astype(BF)

    def tri_linear(kind):
        return mm_nt(tri, tw[:, kind].reshape(128, 128))

    tr_scr[...] = jax.nn.sigmoid(tri_linear(3)) * tri_linear(2)
    for jj in range(4):
        tr_send[16 * jj : 16 * jj + 16, :] = tr_scr[
            pl.ds(4 * (b % 2) + jj, 16, stride=8), :
        ].astype(BF)
    send_right(tr_send, trbuf, s_tr)
    tl_send[...] = (jax.nn.sigmoid(tri_linear(1)) * tri_linear(0)).astype(BF)
    send_group("col", c, NC, lambda peer: tl_send, tlbuf, s_tl)
    tlbuf[c] = tl_send[...]

    arrived(bb2, NR - 1, s_b2)
    bias = bb2[...].astype(F32)
    head_lane = iota((128, 64), 1) // DEPTH
    wide_lane = (iota((128, 128), 1) % 64) // DEPTH
    contexts = []
    for s in range(2):
        q = aq[s]
        context = jnp.zeros((128, 128), F32)
        for h in range(HEADS):
            qh = jnp.where(head_lane == h, q, jnp.zeros_like(q))
            scores = mm_nt(qh, ak[s]) * (float(DEPTH) ** -0.5)
            scores = scores + bias[:, 8 * h : 8 * h + 8].reshape(128, 128)
            expo = jnp.exp(scores - jnp.max(scores, axis=-1, keepdims=True))
            total = jnp.sum(expo, axis=-1, keepdims=True)
            context = jnp.where(wide_lane == h, mm(expo.astype(BF), av[s]) / total, context)
        context = context * jax.nn.sigmoid(ag[s])
        contexts.append(context.reshape(16, 8, 128))
    ctx_send[...] = jnp.concatenate(contexts, axis=1).astype(BF)
    send_group("row", r, NR, lambda peer: ctx_send.at[peer], cb, s_c)
    cb[r] = ctx_send[r]

    loads["close"].wait()
    loads["change"].wait()
    loads["wf"].wait()
    own_normed = standardise(mid.astype(F32)).astype(BF)
    closing = jax.nn.sigmoid(mm(own_normed, w_close[...]))
    half = iota((16, 8, 128), 2) < 64
    choose = (iota((256, 128), 0) == 64 * b + iota((256, 128), 1) % 64).astype(BF)
    own = mm(hom[...], choose).reshape(16, 2, 8, 128)
    own = jnp.where(half, own[:, 0], own[:, 1]).reshape(128, 128)

    arrived(cb, NR - 1, s_c)
    ctx = cb[...].astype(F32).reshape(256, 128).astype(BF)
    full = mm(ctx[:, :64], wf[...])
    for n in range(0, NB, 2):
        part = full[:, 64 * n : 64 * n + 128]
        swapped = pltpu.roll(part, 64, 1).reshape(16, 2, 8, 128)
        part = part.reshape(16, 2, 8, 128)
        first = jnp.where(half, part[:, 0], swapped[:, 1])
        second = jnp.where(half, swapped[:, 0], part[:, 1])
        p_send[n] = first.reshape(128, 128).astype(BF)
        p_send[n + 1] = second.reshape(128, 128).astype(BF)
    send_group("branch", b, NB, lambda peer: p_send.at[peer], pbuf, s_p)
    pbuf[b] = p_send[b]

    arrived(tlbuf, NC - 1, s_tl)
    arrived(trbuf, NC, s_tr)
    tlf[...] = tlbuf[...].astype(F32)
    trf[...] = trbuf[...].astype(F32)

    def product_step(k, acc):
        acc = list(acc)
        for kk in range(16):
            t = tlf[k, 8 * kk : 8 * kk + 8, :]
            for j in range(4):
                acc[j] = acc[j] + t * trf[k, 16 * j + kk : 16 * j + kk + 1, :]
        return tuple(acc)

    product = lax.fori_loop(
        0, NC, product_step, tuple(jnp.zeros((8, 128), F32) for _ in range(4))
    )
    product_normed = standardise(jnp.concatenate(product, axis=0)).astype(BF)
    change = mm(product_normed, w_change[...])
    obuf[b] = (mid.astype(F32) + closing * change).astype(BF)
    send_group("branch", b, NB, lambda peer: obuf.at[b], obuf, s_o)

    arrived(pbuf, NB - 1, s_p)
    msa = own + jnp.sum(pbuf[...].astype(F32), axis=0)
    msa_out[:, 0] = msa[:, :64].reshape(16, 8, 64).astype(BF)
    msa_out[:, 1] = pltpu.roll(msa, 64, 1)[:, :64].reshape(16, 8, 64).astype(BF)
    left_device(lbuf, NC - 1, s_l)
    left_right(rbuf, s_r)
    left_device(bb1, NC - 1, s_b1)
    left_device(xa, NR - 1, s_x)
    left_device(tw, NB - 1, s_w)
    left_device(bb2, NR - 1, s_b2)
    left_device(midbuf, NB - 1, s_mid)
    left_device(tlbuf, NC - 1, s_tl)
    left_right(trbuf, s_tr)
    left_device(cb, NR - 1, s_c)
    left_device(pbuf, NB - 1, s_p)
    arrived(obuf, NB - 1, s_o)
    tr_scr[...] = obuf[...].astype(F32).reshape(128, 128)
    for i in range(8):
        pair_out[i] = tr_scr[pl.ds(i, 16, stride=8), :].astype(BF)
    left_device(obuf, NB - 1, s_o)


def per_device(
    homolog_tensor,
    couple_tensor,
    probe_matrix,
    lookup_matrix,
    content_matrix,
    scoring_sigmoid_matrix,
    scoring_final_matrix,
    couple_offset_matrix,
    product_first_matrix,
    product_second_matrix,
    product_final_matrix,
    trio_first_matrix,
    trio_second_matrix,
    trio_sigmoid_matrix,
    trio_final_matrix,
):
    operands = (
        homolog_tensor.reshape(256, 256),
        couple_tensor.reshape(128, 128),
        probe_matrix.T,
        lookup_matrix.T,
        content_matrix.T,
        scoring_sigmoid_matrix.T,
        scoring_final_matrix,
        couple_offset_matrix.T,
        product_first_matrix.T,
        product_second_matrix.T,
        product_final_matrix,
        jnp.transpose(trio_first_matrix, (0, 2, 1)),
        jnp.transpose(trio_second_matrix, (0, 2, 1)),
        trio_sigmoid_matrix,
        trio_final_matrix,
    )
    vmem = pl.BlockSpec(memory_space=pltpu.VMEM)
    scratch = [
        ((256, 256), BF),
        ((128, 128), BF),
        ((64, 256), BF),
        ((64, 256), BF),
        ((64, 256), BF),
        ((64, 256), BF),
        ((64, 256), BF),
        ((2, 128), BF),
        ((32, 256), BF),
        ((32, 256), BF),
        ((1024, 128), BF),
        ((128, 128), BF),
        ((128, 128), BF),
        ((32, 256), BF),
        ((8, 32, 256), BF),
        ((32, 128), BF),
        ((8, 32, 128), BF),
        ((16, 16, 256), BF),
        ((16, 128), BF),
        ((8, 16, 128), BF),
        ((16, 128), BF),
        ((16, 16, 128), BF),
        ((4, 4, 32, 128), BF),
        ((4, 32, 128), BF),
        ((128, 128), F32),
        ((128, 128), BF),
        ((8, 128, 128), BF),
        ((128, 128), F32),
        ((64, 128), BF),
        ((8, 64, 128), BF),
        ((8, 128, 128), F32),
        ((8, 64, 128), F32),
        ((4, 32, 128), BF),
        ((16, 16, 128), BF),
        ((16, 16, 128), BF),
        ((4, 128, 128), BF),
        ((4, 128, 128), BF),
        ((2, 128, 64), BF),
        ((2, 128, 64), BF),
        ((2, 128, 128), BF),
        ((2, 128, 128), F32),
    ]
    msa, pairwise = pl.pallas_call(
        kernel,
        out_shape=(
            jax.ShapeDtypeStruct((16, 2, 8, 64), BF),
            jax.ShapeDtypeStruct((8, 16, 128), BF),
        ),
        in_specs=[pl.BlockSpec(memory_space=pltpu.HBM)] * len(operands),
        out_specs=(vmem, vmem),
        scratch_shapes=[pltpu.VMEM(*s) for s in scratch]
        + [pltpu.SemaphoreType.DMA((len(operands),))]
        + [pltpu.SemaphoreType.DMA((2,))] * 12,
        compiler_params=pltpu.CompilerParams(
            collective_id=0, has_side_effects=True
        ),
        name="block",
    )(*operands)
    return (msa.reshape(32, 8, 64), pairwise)


def solution(mesh):
    return jax.shard_map(
        per_device,
        mesh=mesh,
        in_specs=(
            P("col", "row", None),
            P("row", "col", None),
            P(None, "branch"),
            P(None, "branch"),
            P(None, "branch"),
            P(None, "branch"),
            P("branch", None),
            P(None, "branch"),
            P(),
            P(),
            P(),
            P(None, None, "branch"),
            P(None, None, "branch"),
            P(),
            P(),
        ),
        out_specs=(P("col", "row", "branch"), P("row", "col", None)),
        check_vma=False,
    )
```

time: 53.5 us -> 45.5 us (0.85)
  local copies, waits for them, and re-layouts: 8.85 us -> 2.1 us
    unnamed x34 -> x4, local copies, waits for them, and re-layouts: 7.16 us -> 2.1 us
    reshape x7 -> x0, local copies, waits for them, and re-layouts: 0.94 us -> none  [the longest x1 0.62 us: per_device(): pairwise = jnp.transpose(pair.reshape(16, 8, 128), (1, 0, 2))]
    transpose x2 -> x0, local copies, waits for them, and re-layouts: 0.65 us -> none  [the longest x1 0.64 us: per_device(): jnp.transpose(msa.reshape(16, 8, 2, 64), (0, 2, 1, 3)).reshape(32, 8, 64)]
where the time goes in v2:
time: 45.5 us; the launch traced here: 45.3 us
  Pallas kernels  42.6 us (94%)
  local copies, waits for them, and re-layouts  2.1 us (5%)
  between operations  0.65 us (1%)
    pallas_call x1, Pallas kernels, per_device(): pl.pallas_call(kernel, out_shape=(jax.ShapeDtypeStruct((16, 2, 8, 64), BF...  42.6 us
    unnamed x4, local copies, waits for them, and re-layouts  2.1 us

profile of v2, /device:TPU:1, one launch (start us, length us, event | category | flops | bytes accessed | tf_op | source)
XLA Modules:
  0.0 45.3 jit_solution(18120405748591013786)
XLA Ops:
  0.6 42.6 %block.1 = (bf16[16,2,8,64]{3,2,1,0:T(8,128)(2,1)}, bf16[8,16,128]{2,1,0:T(8,128)(2,1)}) custom-call(bf16[256,256]{1,0:T(8,128)(2,1)} %bitcast.12, bf16[128,128]{1,0:T(8,128)(2,1)} %bitcast.14, bf16[64,256]{1,0:T(8,128)(2,1)} %bitcast.15, bf16[64,256]{1,0:T(8,128)(2,1)} %bitcast.16, bf16[64,256]{1,0:T(8,128)(2,1)} %bitcast.17, bf16[64,256]{1,0:T(8,128)(2,1)} %bitcast.18, ...), custom_call_target="tpu_custom_call" | custom-call | tf_op jit(solution)/shard_map/block/pallas_call | solution.py:448
  43.2 0.0 copy-start
  43.2 1.5 %copy.19 = bf16[32,8,64]{2,1,0:T(8,128)(2,1)} copy(bf16[32,8,64]{2,1,0:T(8,128)(2,1)} %bitcast.13) | data formatting | bytes 65536
  44.7 0.0 copy-done
  44.7 0.6 %copy.20 = bf16[8,16,128]{2,1,0:T(8,128)(2,1)} copy(bf16[8,16,128]{2,1,0:T(8,128)(2,1)S(1)} %copy-done) | data formatting | bytes 65536
Async XLA Ops:
  43.2 1.5 %copy-start = (bf16[8,16,128]{2,1,0:T(8,128)(2,1)S(1)}, bf16[8,16,128]{2,1,0:T(8,128)(2,1)}, u32[]{:S(2)}) copy-start(bf16[8,16,128]{2,1,0:T(8,128)(2,1)} %get-tuple-element.9) | copy-start | bytes 98308

commit v3 on v2

--- a/solution.py
+++ b/solution.py
@@ -51,7 +51,7 @@
     l_send, lbuf, r_send, rbuf, xa, b_send, bb1, b2_send, bb2, tw, midbuf, coup_f,
     tl_send, tlbuf, tr_scr, tr_send, trbuf, tlf, trf, obuf,
     ctx_send, cb, p_send, pbuf, aq, ak, av, ag,
-    s_in, s_l, s_r, s_x, s_b1, s_b2, s_w, s_mid, s_tl, s_tr, s_o, s_c, s_p,
+    s_in, s_l, s_r, s_x, s_b1, s_b2, s_w, s_mid, s_tl, s_tr, s_o, s_c, s_p, s_rd, s_trd,
 ):
     b = lax.axis_index("branch")
     r = lax.axis_index("row")
@@ -59,7 +59,9 @@
     active = (b // 2) == (r % 2)
     c_dest = r // 2
     r_src = 2 * c + b // 2
-    same_col = c_dest == c
+    core = r % 2
+    to_core = c % 2
+    to_self = jnp.logical_and(c_dest == c, core == to_core)
 
     loads = {
         name: pltpu.make_async_copy(source, dest, s_in.at[n])
@@ -105,33 +107,17 @@
     greet("branch", b, NB)
 
     def greet_source(k, _):
-        @pl.when(jnp.logical_or(r_src != r, k != c))
+        source_col = 2 * k + core
+
+        @pl.when(jnp.logical_or(r_src != r, source_col != c))
         def _():
             pl.semaphore_signal(
-                barrier, inc=1, device_id={"row": r_src, "col": k}, device_id_type=MESH
+                barrier, inc=1, device_id={"row": r_src, "col": source_col}, device_id_type=MESH
             )
 
         return 0
 
-    lax.fori_loop(0, NC, greet_source, 0)
-
-    loads["wl"].wait()
-    loads["wr"].wait()
-    spread = (iota((256, 32), 0) // 8 == iota((256, 32), 1)).astype(BF)
-    wl_wide = mm(spread, wl[...]).astype(BF)
-    wr_wide = jnp.concatenate([wr[...]] * 8, axis=0)
-    row_i = iota((256, 256), 0) % 8
-    lane = iota((256, 256), 1)
-    pick = (iota((32, 256), 1) // 8 == iota((32, 256), 0)).astype(BF)
-    loads["hom"].wait()
-    normed = standardise(hom[...].astype(F32)).astype(BF)
-    left = jnp.where(lane % 8 == row_i, mm_nt(normed, wl_wide), 0.0).astype(BF)
-    right = jnp.where(lane // 32 == row_i, mm_nt(normed, wr_wide), 0.0).astype(BF)
-    l_send[...] = mm(pick, left).astype(BF)
-    right = mm(pick, right).astype(BF)
-    r_send[...] = jnp.where(b % 2 == 0, right[:, :128], right[:, 128:])
-
-    pl.semaphore_wait(barrier, 25 + jnp.where(active, jnp.where(same_col, 15, 16), 0))
+    lax.fori_loop(0, NC // 2, greet_source, 0)
 
     def send_group(axis, me, size, source, dest, sems):
         def body(d, _):
@@ -148,28 +134,52 @@
 
         lax.fori_loop(1, size, body, 0)
 
-    def send_right(source, dest, sems):
+    def for_right(body):
         @pl.when(active)
         def _():
-            def body(peer, _):
-                @pl.when(jnp.logical_or(peer != r, jnp.logical_not(same_col)))
+            def step(chip, _):
+                peer = 2 * chip + to_core
+
+                @pl.when(jnp.logical_or(peer != r, c_dest != c))
                 def _():
-                    pltpu.make_async_remote_copy(
-                        src_ref=source,
-                        dst_ref=dest.at[c],
-                        send_sem=sems.at[0],
-                        recv_sem=sems.at[1],
-                        device_id={"row": peer, "col": c_dest},
-                        device_id_type=MESH,
-                    ).start()
+                    body(peer)
 
                 return 0
 
-            lax.fori_loop(0, NR, body, 0)
-
-            @pl.when(same_col)
-            def _():
-                pltpu.make_async_copy(source, dest.at[c], sems.at[1]).start()
+            lax.fori_loop(0, NR // 2, step, 0)
+
+    def send_right(source, dest, sems, direct):
+        def send(peer):
+            pltpu.make_async_remote_copy(
+                src_ref=source,
+                dst_ref=dest.at[c],
+                send_sem=sems.at[2],
+                recv_sem=direct.at[c],
+                device_id={"row": peer, "col": c_dest},
+                device_id_type=MESH,
+            ).start()
+
+        for_right(send)
+
+        @pl.when(jnp.logical_and(active, to_self))
+        def _():
+            pltpu.make_async_copy(source, dest.at[c], direct.at[c]).start()
+
+    def forward_right(dest, sems, direct):
+        def step(k, _):
+            block = 2 * k + core
+            wait_bytes(dest.at[block], direct.at[block])
+            pltpu.make_async_remote_copy(
+                src_ref=dest.at[block],
+                dst_ref=dest.at[block],
+                send_sem=sems.at[0],
+                recv_sem=sems.at[1],
+                device_id={"row": r + 1 - 2 * core},
+                device_id_type=MESH,
+            ).start()
+            return 0
+
+        lax.fori_loop(0, NC // 2, step, 0)
 
     def wait_bytes(ref, sem):
         pltpu.make_async_copy(ref, ref, sem).wait()
@@ -181,20 +191,35 @@
         wait_bytes(dest.at[pl.ds(0, size)], sems.at[0])
 
     def left_right(dest, sems):
-        @pl.when(active)
-        def _():
-            def body(peer, _):
-                @pl.when(jnp.logical_or(peer != r, jnp.logical_not(same_col)))
-                def _():
-                    wait_bytes(dest.at[0], sems.at[0])
-
-                return 0
-
-            lax.fori_loop(0, NR, body, 0)
-
-    send_right(r_send, rbuf, s_r)
+        left_device(dest, NC // 2, sems)
+        for_right(lambda peer: wait_bytes(dest.at[0], sems.at[2]))
+
+    loads["wl"].wait()
+    loads["wr"].wait()
+    spread = (iota((256, 32), 0) // 8 == iota((256, 32), 1)).astype(BF)
+    wl_wide = mm(spread, wl[...]).astype(BF)
+    wr_wide = jnp.concatenate([wr[...]] * 8, axis=0)
+    row_i = iota((256, 256), 0) % 8
+    lane = iota((256, 256), 1)
+    pick = (iota((32, 256), 1) // 8 == iota((32, 256), 0)).astype(BF)
+
+    pl.semaphore_wait(barrier, 25 + jnp.where(active, jnp.where(to_self, 7, 8), 0))
+    send_group("row", r, NR, lambda peer: hom_hbm.at[pl.ds(16 * peer, 16)], xa, s_x)
+    loads["hom"].wait()
+    normed = standardise(hom[...].astype(F32)).astype(BF)
+    left = jnp.where(lane % 8 == row_i, mm_nt(normed, wl_wide), 0.0).astype(BF)
+    right = jnp.where(lane // 32 == row_i, mm_nt(normed, wr_wide), 0.0).astype(BF)
+    l_send[...] = mm(pick, left).astype(BF)
+    right = mm(pick, right).astype(BF)
+    r_send[...] = jnp.where(b % 2 == 0, right[:, :128], right[:, 128:])
+
+    send_right(r_send, rbuf, s_r, s_rd)
     send_group("col", c, NC, lambda peer: l_send, lbuf, s_l)
     lbuf[c] = l_send[...]
+    xa[r] = hom[pl.ds(pl.multiple_of(16 * r, 16), 16), :]
+    loads["t1"].wait()
+    loads["t2"].wait()
+    send_group("branch", b, NB, lambda peer: tw.at[b], tw, s_w)
 
     loads["coup"].wait()
     loads["wo"].wait()
@@ -214,18 +239,34 @@
     b_send[...] = mm(tile.astype(BF), place).astype(BF)
     send_group("col", c, NC, lambda peer: b_send, bb1, s_b1)
     bb1[c] = b_send[...]
-    send_group("row", r, NR, lambda peer: hom.at[pl.ds(16 * peer, 16)], xa, s_x)
-    xa[r] = hom[pl.ds(pl.multiple_of(16 * r, 16), 16), :]
-    loads["t1"].wait()
-    loads["t2"].wait()
-    send_group("branch", b, NB, lambda peer: tw.at[b], tw, s_w)
     coup_own = jnp.concatenate(
         [coup_f[pl.ds(4 * b + j, 8, stride=16), :] for j in range(4)], axis=0
     )
 
+    for name in ("wq", "wk", "wv", "wg"):
+        loads[name].wait()
+    arrived(xa, NR - 1, s_x)
+    att_normed = standardise(xa[...].astype(F32).reshape(256, 256)).astype(BF)
+
+    def by_row(weights, dest):
+        y = mm_nt(att_normed, weights).reshape(16, 2, 8, -1)
+        for s in range(2):
+            dest[s] = y[:, s].reshape(128, -1).astype(dest.dtype)
+
+    by_row(wq[...], aq)
+    by_row(wk[...], ak)
+    by_row(jnp.concatenate([wv[...]] * 2, axis=0), av)
+    by_row(jnp.concatenate([wg[...]] * 2, axis=0), ag)
+
+    arrived(bb1, NC - 1, s_b1)
+    b2_send[...] = jnp.sum(bb1[...].astype(F32), axis=0).astype(BF)
+    send_group("row", r, NR, lambda peer: b2_send, bb2, s_b2)
+    bb2[r] = b2_send[...]
+
     loads["prod"].wait()
     arrived(lbuf, NC - 1, s_l)
-    arrived(rbuf, NC, s_r)
+    forward_right(rbuf, s_r, s_rd)
+    arrived(rbuf, NC // 2, s_r)
     outer = mm_tn(lbuf[...].reshape(256, 256), rbuf[...].reshape(256, 128))
     turned = [outer] + [pltpu.roll(outer, 32 * k, 1) for k in range(1, 4)]
     turned = [t.reshape(8, 4, 8, 128) for t in turned]
@@ -241,43 +282,6 @@
     mid = (coup_own + update).astype(BF)
     midbuf[b] = mid
     send_group("branch", b, NB, lambda peer: midbuf.at[b], midbuf, s_mid)
-
-    arrived(bb1, NC - 1, s_b1)
-    b2_send[...] = jnp.sum(bb1[...].astype(F32), axis=0).astype(BF)
-    send_group("row", r, NR, lambda peer: b2_send, bb2, s_b2)
-    bb2[r] = b2_send[...]
-
-    for name in ("wq", "wk", "wv", "wg"):
-        loads[name].wait()
-    arrived(xa, NR - 1, s_x)
-    att_normed = standardise(xa[...].astype(F32).reshape(256, 256)).astype(BF)
-
-    def by_row(weights, dest):
-        y = mm_nt(att_normed, weights).reshape(16, 2, 8, -1)
-        for s in range(2):
-            dest[s] = y[:, s].reshape(128, -1).astype(dest.dtype)
-
-    by_row(wq[...], aq)
-    by_row(wk[...], ak)
-    by_row(jnp.concatenate([wv[...]] * 2, axis=0), av)
-    by_row(jnp.concatenate([wg[...]] * 2, axis=0), ag)
-
-    arrived(tw, NB - 1, s_w)
-    arrived(midbuf, NB - 1, s_mid)
-    tri = standardise(midbuf[...].astype(F32).reshape(128, 128)).astype(BF)
-
-    def tri_linear(kind):
-        return mm_nt(tri, tw[:, kind].reshape(128, 128))
-
-    tr_scr[...] = jax.nn.sigmoid(tri_linear(3)) * tri_linear(2)
-    for jj in range(4):
-        tr_send[16 * jj : 16 * jj + 16, :] = tr_scr[
-            pl.ds(4 * (b % 2) + jj, 16, stride=8), :
-        ].astype(BF)
-    send_right(tr_send, trbuf, s_tr)
-    tl_send[...] = (jax.nn.sigmoid(tri_linear(1)) * tri_linear(0)).astype(BF)
-    send_group("col", c, NC, lambda peer: tl_send, tlbuf, s_tl)
-    tlbuf[c] = tl_send[...]
 
     arrived(bb2, NR - 1, s_b2)
     bias = bb2[...].astype(F32)
@@ -300,6 +304,23 @@
     send_group("row", r, NR, lambda peer: ctx_send.at[peer], cb, s_c)
     cb[r] = ctx_send[r]
 
+    arrived(tw, NB - 1, s_w)
+    arrived(midbuf, NB - 1, s_mid)
+    tri = standardise(midbuf[...].astype(F32).reshape(128, 128)).astype(BF)
+
+    def tri_linear(kind):
+        return mm_nt(tri, tw[:, kind].reshape(128, 128))
+
+    tr_scr[...] = jax.nn.sigmoid(tri_linear(3)) * tri_linear(2)
+    for jj in range(4):
+        tr_send[16 * jj : 16 * jj + 16, :] = tr_scr[
+            pl.ds(4 * (b % 2) + jj, 16, stride=8), :
+        ].astype(BF)
+    send_right(tr_send, trbuf, s_tr, s_trd)
+    tl_send[...] = (jax.nn.sigmoid(tri_linear(1)) * tri_linear(0)).astype(BF)
+    send_group("col", c, NC, lambda peer: tl_send, tlbuf, s_tl)
+    tlbuf[c] = tl_send[...]
+
     loads["close"].wait()
     loads["change"].wait()
     loads["wf"].wait()
@@ -324,8 +345,9 @@
     send_group("branch", b, NB, lambda peer: p_send.at[peer], pbuf, s_p)
     pbuf[b] = p_send[b]
 
+    forward_right(trbuf, s_tr, s_trd)
     arrived(tlbuf, NC - 1, s_tl)
-    arrived(trbuf, NC, s_tr)
+    arrived(trbuf, NC // 2, s_tr)
     tlf[...] = tlbuf[...].astype(F32)
     trf[...] = trbuf[...].astype(F32)
 
@@ -455,7 +477,8 @@
         out_specs=(vmem, vmem),
         scratch_shapes=[pltpu.VMEM(*s) for s in scratch]
         + [pltpu.SemaphoreType.DMA((len(operands),))]
-        + [pltpu.SemaphoreType.DMA((2,))] * 12,
+        + [pltpu.SemaphoreType.DMA((3,))] * 12
+        + [pltpu.SemaphoreType.DMA((NC,))] * 2,
         compiler_params=pltpu.CompilerParams(
             collective_id=0, has_side_effects=True
         ),

time: 45.5 us -> 46.3 us (1.018)
  Pallas kernels: 42.6 us -> 43.4 us
    pallas_call x1, Pallas kernels: 42.6 us -> 43.4 us  [per_device(): pl.pallas_call(kernel, out_shape=(jax.ShapeDtypeStruct((16, 2, 8, 64), BF...]
where the time goes in v3:
time: 46.3 us; the launch traced here: 46.1 us
  Pallas kernels  43.4 us (94%)
  local copies, waits for them, and re-layouts  2.1 us (5%)
  between operations  0.65 us (1%)
    pallas_call x1, Pallas kernels, per_device(): pl.pallas_call(kernel, out_shape=(jax.ShapeDtypeStruct((16, 2, 8, 64), BF...  43.4 us
    unnamed x4, local copies, waits for them, and re-layouts  2.1 us

profile of v3, /device:TPU:1, one launch (start us, length us, event | category | flops | bytes accessed | tf_op | source)
XLA Modules:
  0.0 46.1 jit_solution(13377921069657556812)
XLA Ops:
  0.6 43.4 %block.1 = (bf16[16,2,8,64]{3,2,1,0:T(8,128)(2,1)}, bf16[8,16,128]{2,1,0:T(8,128)(2,1)}) custom-call(bf16[256,256]{1,0:T(8,128)(2,1)} %bitcast.12, bf16[128,128]{1,0:T(8,128)(2,1)} %bitcast.14, bf16[64,256]{1,0:T(8,128)(2,1)} %bitcast.15, bf16[64,256]{1,0:T(8,128)(2,1)} %bitcast.16, bf16[64,256]{1,0:T(8,128)(2,1)} %bitcast.17, bf16[64,256]{1,0:T(8,128)(2,1)} %bitcast.18, ...), custom_call_target="tpu_custom_call" | custom-call | tf_op jit(solution)/shard_map/block/pallas_call | solution.py:470
  44.0 0.0 copy-start
  44.0 1.5 %copy.19 = bf16[32,8,64]{2,1,0:T(8,128)(2,1)} copy(bf16[32,8,64]{2,1,0:T(8,128)(2,1)} %bitcast.13) | data formatting | bytes 65536
  45.5 0.0 copy-done
  45.5 0.6 %copy.20 = bf16[8,16,128]{2,1,0:T(8,128)(2,1)} copy(bf16[8,16,128]{2,1,0:T(8,128)(2,1)S(1)} %copy-done) | data formatting | bytes 65536
Async XLA Ops:
  44.0 1.5 %copy-start = (bf16[8,16,128]{2,1,0:T(8,128)(2,1)S(1)}, bf16[8,16,128]{2,1,0:T(8,128)(2,1)}, u32[]{:S(2)}) copy-start(bf16[8,16,128]{2,1,0:T(8,128)(2,1)} %get-tuple-element.9) | copy-start | bytes 98308

commit v4 on v2

--- a/solution.py
+++ b/solution.py
@@ -47,18 +47,17 @@
     close_hbm, change_hbm,
     msa_out,
     pair_out,
-    hom, coup, wq, wk, wv, wg, wf, wo, wl, wr, w_prod, w_close, w_change,
-    l_send, lbuf, r_send, rbuf, xa, b_send, bb1, b2_send, bb2, tw, midbuf, coup_f,
-    tl_send, tlbuf, tr_scr, tr_send, trbuf, tlf, trf, obuf,
-    ctx_send, cb, p_send, pbuf, aq, ak, av, ag,
-    s_in, s_l, s_r, s_x, s_b1, s_b2, s_w, s_mid, s_tl, s_tr, s_o, s_c, s_p,
+    hom, coup, wq, wk, wv, wg, wo, wl, wr, w_prod, w_close, w_change,
+    l_send, lbuf, r_send, rbuf, xa, b_send, bb1, b2_send, bb2, tw, wfall, midbuf, coup_f,
+    tl_send, tlbuf, tr_send, trbuf, tlf, trf, p_send, pbuf, tile_f,
+    ctx_send, cb, aq, ak, av, ag,
+    s_in, s_l, s_r, s_x, s_b1, s_b2, s_w, s_wf, s_mid, s_tl, s_tr, s_c, s_p,
 ):
     b = lax.axis_index("branch")
     r = lax.axis_index("row")
     c = lax.axis_index("col")
     active = (b // 2) == (r % 2)
     c_dest = r // 2
-    r_src = 2 * c + b // 2
     same_col = c_dest == c
 
     loads = {
@@ -79,13 +78,10 @@
                 ("wg", wg_hbm, wg),
                 ("close", close_hbm, w_close),
                 ("change", change_hbm, w_change),
-                ("wf", wf_hbm, wf),
+                ("wf", wf_hbm, wfall.at[b]),
             )
         )
     }
-    for name in loads:
-        loads[name].start()
-
     barrier = pltpu.get_barrier_semaphore()
 
     def wrapped(value, size):
@@ -100,20 +96,37 @@
 
         lax.fori_loop(1, size, body, 0)
 
+    def greet_diagonal(d, _):
+        for e in range(1, NB):
+            pl.semaphore_signal(
+                barrier,
+                inc=1,
+                device_id={"branch": wrapped(b + e, NB), "row": wrapped(r + d, NR)},
+                device_id_type=MESH,
+            )
+        return 0
+
+    def greet_source(k, _):
+        for half in range(2):
+            @pl.when(jnp.logical_or(2 * c + half != r, k != c))
+            def _():
+                pl.semaphore_signal(
+                    barrier,
+                    inc=1,
+                    device_id={"row": 2 * c + half, "col": k},
+                    device_id_type=MESH,
+                )
+
+        return 0
+
+    loads["hom"].start()
+    lax.fori_loop(0, NC, greet_source, 0)
+    lax.fori_loop(1, NR, greet_diagonal, 0)
     greet("row", r, NR)
+    greet("branch", b, NB)
     greet("col", c, NC)
-    greet("branch", b, NB)
-
-    def greet_source(k, _):
-        @pl.when(jnp.logical_or(r_src != r, k != c))
-        def _():
-            pl.semaphore_signal(
-                barrier, inc=1, device_id={"row": r_src, "col": k}, device_id_type=MESH
-            )
-
-        return 0
-
-    lax.fori_loop(0, NC, greet_source, 0)
+    for name in list(loads)[1:]:
+        loads[name].start()
 
     loads["wl"].wait()
     loads["wr"].wait()
@@ -131,7 +144,7 @@
     right = mm(pick, right).astype(BF)
     r_send[...] = jnp.where(b % 2 == 0, right[:, :128], right[:, 128:])
 
-    pl.semaphore_wait(barrier, 25 + jnp.where(active, jnp.where(same_col, 15, 16), 0))
+    pl.semaphore_wait(barrier, 15 + 7 + 3 + 45 + jnp.where(same_col, 15, 16))
 
     def send_group(axis, me, size, source, dest, sems):
         def body(d, _):
@@ -148,28 +161,32 @@
 
         lax.fori_loop(1, size, body, 0)
 
-    def send_right(source, dest, sems):
-        @pl.when(active)
+    def for_transposed(body):
+        def step(peer, _):
+            @pl.when(jnp.logical_or(peer != r, jnp.logical_not(same_col)))
+            def _():
+                body(peer)
+
+            return 0
+
+        lax.fori_loop(0, NR, step, 0)
+
+    def send_transposed(source, dest, sems):
+        def send(peer):
+            pltpu.make_async_remote_copy(
+                src_ref=source,
+                dst_ref=dest,
+                send_sem=sems.at[0],
+                recv_sem=sems.at[1],
+                device_id={"row": peer, "col": c_dest},
+                device_id_type=MESH,
+            ).start()
+
+        for_transposed(send)
+
+        @pl.when(same_col)
         def _():
-            def body(peer, _):
-                @pl.when(jnp.logical_or(peer != r, jnp.logical_not(same_col)))
-                def _():
-                    pltpu.make_async_remote_copy(
-                        src_ref=source,
-                        dst_ref=dest.at[c],
-                        send_sem=sems.at[0],
-                        recv_sem=sems.at[1],
-                        device_id={"row": peer, "col": c_dest},
-                        device_id_type=MESH,
-                    ).start()
-
-                return 0
-
-            lax.fori_loop(0, NR, body, 0)
-
-            @pl.when(same_col)
-            def _():
-                pltpu.make_async_copy(source, dest.at[c], sems.at[1]).start()
+            pltpu.make_async_copy(source, dest, sems.at[1]).start()
 
     def wait_bytes(ref, sem):
         pltpu.make_async_copy(ref, ref, sem).wait()
@@ -180,19 +197,13 @@
     def left_device(dest, size, sems):
         wait_bytes(dest.at[pl.ds(0, size)], sems.at[0])
 
-    def left_right(dest, sems):
-        @pl.when(active)
-        def _():
-            def body(peer, _):
-                @pl.when(jnp.logical_or(peer != r, jnp.logical_not(same_col)))
-                def _():
-                    wait_bytes(dest.at[0], sems.at[0])
-
-                return 0
-
-            lax.fori_loop(0, NR, body, 0)
-
-    send_right(r_send, rbuf, s_r)
+    def left_transposed(ref, sems):
+        for_transposed(lambda peer: wait_bytes(ref, sems.at[0]))
+
+    @pl.when(active)
+    def _():
+        send_transposed(r_send, rbuf.at[c], s_r)
+
     send_group("col", c, NC, lambda peer: l_send, lbuf, s_l)
     lbuf[c] = l_send[...]
 
@@ -219,6 +230,8 @@
     loads["t1"].wait()
     loads["t2"].wait()
     send_group("branch", b, NB, lambda peer: tw.at[b], tw, s_w)
+    loads["wf"].wait()
+    send_group("branch", b, NB, lambda peer: wfall.at[b], wfall, s_wf)
     coup_own = jnp.concatenate(
         [coup_f[pl.ds(4 * b + j, 8, stride=16), :] for j in range(4)], axis=0
     )
@@ -240,6 +253,18 @@
     update = mm(x, w_prod[...]) * (1.0 / 256.0)
     mid = (coup_own + update).astype(BF)
     midbuf[b] = mid
+
+    arrived(tw, NB - 1, s_w)
+    tri = standardise(mid.astype(F32)).astype(BF)
+
+    def tri_linear(kind):
+        return mm_nt(tri, tw[:, kind].reshape(128, 128))
+
+    tr_send[...] = (jax.nn.sigmoid(tri_linear(3)) * tri_linear(2)).astype(BF)
+    send_transposed(tr_send, trbuf.at[r % 2, c], s_tr)
+    tl_send[...] = (jax.nn.sigmoid(tri_linear(1)) * tri_linear(0)).astype(BF)
+    send_group("col", c, NC, lambda peer: tl_send, tlbuf, s_tl)
+    tlbuf[c] = tl_send[...]
     send_group("branch", b, NB, lambda peer: midbuf.at[b], midbuf, s_mid)
 
     arrived(bb1, NC - 1, s_b1)
@@ -261,23 +286,6 @@
     by_row(wk[...], ak)
     by_row(jnp.concatenate([wv[...]] * 2, axis=0), av)
     by_row(jnp.concatenate([wg[...]] * 2, axis=0), ag)
-
-    arrived(tw, NB - 1, s_w)
-    arrived(midbuf, NB - 1, s_mid)
-    tri = standardise(midbuf[...].astype(F32).reshape(128, 128)).astype(BF)
-
-    def tri_linear(kind):
-        return mm_nt(tri, tw[:, kind].reshape(128, 128))
-
-    tr_scr[...] = jax.nn.sigmoid(tri_linear(3)) * tri_linear(2)
-    for jj in range(4):
-        tr_send[16 * jj : 16 * jj + 16, :] = tr_scr[
-            pl.ds(4 * (b % 2) + jj, 16, stride=8), :
-        ].astype(BF)
-    send_right(tr_send, trbuf, s_tr)
-    tl_send[...] = (jax.nn.sigmoid(tri_linear(1)) * tri_linear(0)).astype(BF)
-    send_group("col", c, NC, lambda peer: tl_send, tlbuf, s_tl)
-    tlbuf[c] = tl_send[...]
 
     arrived(bb2, NR - 1, s_b2)
     bias = bb2[...].astype(F32)
@@ -296,75 +304,103 @@
             context = jnp.where(wide_lane == h, mm(expo.astype(BF), av[s]) / total, context)
         context = context * jax.nn.sigmoid(ag[s])
         contexts.append(context.reshape(16, 8, 128))
-    ctx_send[...] = jnp.concatenate(contexts, axis=1).astype(BF)
-    send_group("row", r, NR, lambda peer: ctx_send.at[peer], cb, s_c)
-    cb[r] = ctx_send[r]
+    first_half = iota((16, 8, 128), 2) < 64
+    ctx_send[...] = jnp.where(first_half, contexts[0], contexts[1]).astype(BF)
+
+    def send_context(peer_row, peer_branch):
+        pltpu.make_async_remote_copy(
+            src_ref=ctx_send.at[peer_row],
+            dst_ref=cb.at[b, r],
+            send_sem=s_c.at[0],
+            recv_sem=s_c.at[1],
+            device_id={"branch": peer_branch, "row": peer_row},
+            device_id_type=MESH,
+        ).start()
+
+    def send_contexts(d, _):
+        for e in range(1, NB):
+            send_context(wrapped(r + d, NR), wrapped(b + e, NB))
+        return 0
+
+    def send_own_branch(d, _):
+        send_context(wrapped(r + d, NR), b)
+        return 0
+
+    lax.fori_loop(0, NR, send_contexts, 0)
+    lax.fori_loop(1, NR, send_own_branch, 0)
+    pltpu.make_async_copy(ctx_send.at[r], cb.at[b, r], s_c.at[1]).start()
 
     loads["close"].wait()
     loads["change"].wait()
-    loads["wf"].wait()
-    own_normed = standardise(mid.astype(F32)).astype(BF)
-    closing = jax.nn.sigmoid(mm(own_normed, w_close[...]))
+    arrived(wfall, NB - 1, s_wf)
+    arrived(midbuf, NB - 1, s_mid)
+    mid_all = midbuf[...].astype(F32).reshape(128, 128)
+    closing = jax.nn.sigmoid(mm(standardise(mid_all).astype(BF), w_close[...]))
+    choose = (iota((256, 128), 0) == 64 * b + iota((256, 128), 1) % 64).astype(BF)
+    w_own = mm(wfall[...].reshape(256, 256), choose)
+    lower = iota((64, 128), 1) < 64
+    w_final = []
+    for n in range(NB):
+        w_n = w_own[64 * n : 64 * n + 64]
+        w_final += [jnp.where(lower, w_n, 0.0), jnp.where(lower, 0.0, w_n)]
+    w_final = jnp.concatenate(w_final, axis=0).astype(BF)
     half = iota((16, 8, 128), 2) < 64
-    choose = (iota((256, 128), 0) == 64 * b + iota((256, 128), 1) % 64).astype(BF)
     own = mm(hom[...], choose).reshape(16, 2, 8, 128)
     own = jnp.where(half, own[:, 0], own[:, 1]).reshape(128, 128)
 
-    arrived(cb, NR - 1, s_c)
-    ctx = cb[...].astype(F32).reshape(256, 128).astype(BF)
-    full = mm(ctx[:, :64], wf[...])
-    for n in range(0, NB, 2):
-        part = full[:, 64 * n : 64 * n + 128]
-        swapped = pltpu.roll(part, 64, 1).reshape(16, 2, 8, 128)
-        part = part.reshape(16, 2, 8, 128)
-        first = jnp.where(half, part[:, 0], swapped[:, 1])
-        second = jnp.where(half, swapped[:, 0], part[:, 1])
-        p_send[n] = first.reshape(128, 128).astype(BF)
-        p_send[n + 1] = second.reshape(128, 128).astype(BF)
-    send_group("branch", b, NB, lambda peer: p_send.at[peer], pbuf, s_p)
-    pbuf[b] = p_send[b]
-
     arrived(tlbuf, NC - 1, s_tl)
-    arrived(trbuf, NC, s_tr)
+    wait_bytes(trbuf, s_tr.at[1])
     tlf[...] = tlbuf[...].astype(F32)
     trf[...] = trbuf[...].astype(F32)
 
     def product_step(k, acc):
         acc = list(acc)
-        for kk in range(16):
+        for kk in range(4):
             t = tlf[k, 8 * kk : 8 * kk + 8, :]
-            for j in range(4):
-                acc[j] = acc[j] + t * trf[k, 16 * j + kk : 16 * j + kk + 1, :]
+            for j in range(16):
+                row = 8 * kk + j % 8
+                acc[j] = acc[j] + t * trf[j // 8, k, row : row + 1, :]
         return tuple(acc)
 
     product = lax.fori_loop(
-        0, NC, product_step, tuple(jnp.zeros((8, 128), F32) for _ in range(4))
+        0, NC, product_step, tuple(jnp.zeros((8, 128), F32) for _ in range(16))
     )
-    product_normed = standardise(jnp.concatenate(product, axis=0)).astype(BF)
-    change = mm(product_normed, w_change[...])
-    obuf[b] = (mid.astype(F32) + closing * change).astype(BF)
-    send_group("branch", b, NB, lambda peer: obuf.at[b], obuf, s_o)
-
-    arrived(pbuf, NB - 1, s_p)
-    msa = own + jnp.sum(pbuf[...].astype(F32), axis=0)
+    product = jnp.concatenate(product, axis=0)
+    p_send[...] = product.astype(BF)
+    send_group("branch", b, NB, lambda peer: p_send, pbuf, s_p)
+    pbuf[b] = p_send[...]
+
+    wait_bytes(cb, s_c.at[1])
+    ctx = cb[...].astype(F32).reshape(4, 128, 128)
+    ctx = jnp.concatenate([ctx[n] for n in range(NB)], axis=1).astype(BF)
+    msa = own + mm(ctx, w_final)
     msa_out[:, 0] = msa[:, :64].reshape(16, 8, 64).astype(BF)
     msa_out[:, 1] = pltpu.roll(msa, 64, 1)[:, :64].reshape(16, 8, 64).astype(BF)
+
     left_device(lbuf, NC - 1, s_l)
-    left_right(rbuf, s_r)
+
+    @pl.when(active)
+    def _():
+        left_transposed(r_send, s_r)
+
     left_device(bb1, NC - 1, s_b1)
     left_device(xa, NR - 1, s_x)
     left_device(tw, NB - 1, s_w)
+    left_device(wfall, NB - 1, s_wf)
     left_device(bb2, NR - 1, s_b2)
     left_device(midbuf, NB - 1, s_mid)
     left_device(tlbuf, NC - 1, s_tl)
-    left_right(trbuf, s_tr)
-    left_device(cb, NR - 1, s_c)
+    left_transposed(tr_send, s_tr)
+    for n in range(NB):
+        left_device(cb.at[n], NR if n else NR - 1, s_c)
+
+    arrived(pbuf, NB - 1, s_p)
+    total = jnp.sum(pbuf[...].astype(F32), axis=0)
+    change = mm(standardise(total).astype(BF), w_change[...])
+    tile_f[...] = mid_all + closing * change
+    for i in range(8):
+        pair_out[i] = tile_f[pl.ds(i, 16, stride=8), :].astype(BF)
     left_device(pbuf, NB - 1, s_p)
-    arrived(obuf, NB - 1, s_o)
-    tr_scr[...] = obuf[...].astype(F32).reshape(128, 128)
-    for i in range(8):
-        pair_out[i] = tr_scr[pl.ds(i, 16, stride=8), :].astype(BF)
-    left_device(obuf, NB - 1, s_o)
 
 
 def per_device(
@@ -409,7 +445,6 @@
         ((64, 256), BF),
         ((64, 256), BF),
         ((64, 256), BF),
-        ((64, 256), BF),
         ((2, 128), BF),
         ((32, 256), BF),
         ((32, 256), BF),
@@ -426,20 +461,20 @@
         ((16, 128), BF),
         ((16, 16, 128), BF),
         ((4, 4, 32, 128), BF),
+        ((4, 64, 256), BF),
         ((4, 32, 128), BF),
         ((128, 128), F32),
+        ((32, 128), BF),
+        ((8, 32, 128), BF),
+        ((32, 128), BF),
+        ((2, 8, 32, 128), BF),
+        ((8, 32, 128), F32),
+        ((2, 8, 32, 128), F32),
         ((128, 128), BF),
-        ((8, 128, 128), BF),
+        ((4, 128, 128), BF),
         ((128, 128), F32),
-        ((64, 128), BF),
-        ((8, 64, 128), BF),
-        ((8, 128, 128), F32),
-        ((8, 64, 128), F32),
-        ((4, 32, 128), BF),
-        ((16, 16, 128), BF),
-        ((16, 16, 128), BF),
-        ((4, 128, 128), BF),
-        ((4, 128, 128), BF),
+        ((16, 8, 128), BF),
+        ((4, 16, 8, 128), BF),
         ((2, 128, 64), BF),
         ((2, 128, 64), BF),
         ((2, 128, 128), BF),

time: 45.5 us -> 47.8 us (1.051)
  Pallas kernels: 42.6 us -> 44.8 us
    pallas_call x1, Pallas kernels: 42.6 us -> 44.8 us  [per_device(): pl.pallas_call(kernel, out_shape=(jax.ShapeDtypeStruct((16, 2, 8, 64), BF...]
where the time goes in v4:
time: 47.8 us; the launch traced here: 47.6 us
  Pallas kernels  44.8 us (94%)
  local copies, waits for them, and re-layouts  2.1 us (4%)
  between operations  0.65 us (1%)
    pallas_call x1, Pallas kernels, per_device(): pl.pallas_call(kernel, out_shape=(jax.ShapeDtypeStruct((16, 2, 8, 64), BF...  44.8 us
    unnamed x4, local copies, waits for them, and re-layouts  2.1 us

profile of v4, /device:TPU:1, one launch (start us, length us, event | category | flops | bytes accessed | tf_op | source)
XLA Modules:
  0.0 47.6 jit_solution(7785733399909122062)
XLA Ops:
  0.6 44.8 %block.1 = (bf16[16,2,8,64]{3,2,1,0:T(8,128)(2,1)}, bf16[8,16,128]{2,1,0:T(8,128)(2,1)}) custom-call(bf16[256,256]{1,0:T(8,128)(2,1)} %bitcast.12, bf16[128,128]{1,0:T(8,128)(2,1)} %bitcast.14, bf16[64,256]{1,0:T(8,128)(2,1)} %bitcast.15, bf16[64,256]{1,0:T(8,128)(2,1)} %bitcast.16, bf16[64,256]{1,0:T(8,128)(2,1)} %bitcast.17, bf16[64,256]{1,0:T(8,128)(2,1)} %bitcast.18, ...), custom_call_target="tpu_custom_call" | custom-call | tf_op jit(solution)/shard_map/block/pallas_call | solution.py:483
  45.5 0.0 copy-start
  45.5 1.5 %copy.19 = bf16[32,8,64]{2,1,0:T(8,128)(2,1)} copy(bf16[32,8,64]{2,1,0:T(8,128)(2,1)} %bitcast.13) | data formatting | bytes 65536
  47.0 0.0 copy-done
  47.0 0.6 %copy.20 = bf16[8,16,128]{2,1,0:T(8,128)(2,1)} copy(bf16[8,16,128]{2,1,0:T(8,128)(2,1)S(1)} %copy-done) | data formatting | bytes 65536
Async XLA Ops:
  45.5 1.5 %copy-start = (bf16[8,16,128]{2,1,0:T(8,128)(2,1)S(1)}, bf16[8,16,128]{2,1,0:T(8,128)(2,1)}, u32[]{:S(2)}) copy-start(bf16[8,16,128]{2,1,0:T(8,128)(2,1)} %get-tuple-element.9) | copy-start | bytes 98308

commit v5 on v4

--- a/solution.py
+++ b/solution.py
@@ -96,16 +96,6 @@
 
         lax.fori_loop(1, size, body, 0)
 
-    def greet_diagonal(d, _):
-        for e in range(1, NB):
-            pl.semaphore_signal(
-                barrier,
-                inc=1,
-                device_id={"branch": wrapped(b + e, NB), "row": wrapped(r + d, NR)},
-                device_id_type=MESH,
-            )
-        return 0
-
     def greet_source(k, _):
         for half in range(2):
             @pl.when(jnp.logical_or(2 * c + half != r, k != c))
@@ -119,13 +109,13 @@
 
         return 0
 
-    loads["hom"].start()
+    for name in ("hom", "wl", "wr"):
+        loads[name].start()
     lax.fori_loop(0, NC, greet_source, 0)
-    lax.fori_loop(1, NR, greet_diagonal, 0)
     greet("row", r, NR)
     greet("branch", b, NB)
     greet("col", c, NC)
-    for name in list(loads)[1:]:
+    for name in list(loads)[3:]:
         loads[name].start()
 
     loads["wl"].wait()
@@ -144,7 +134,7 @@
     right = mm(pick, right).astype(BF)
     r_send[...] = jnp.where(b % 2 == 0, right[:, :128], right[:, 128:])
 
-    pl.semaphore_wait(barrier, 15 + 7 + 3 + 45 + jnp.where(same_col, 15, 16))
+    pl.semaphore_wait(barrier, 15 + 7 + 3 + jnp.where(same_col, 15, 16))
 
     def send_group(axis, me, size, source, dest, sems):
         def body(d, _):
@@ -205,6 +195,7 @@
         send_transposed(r_send, rbuf.at[c], s_r)
 
     send_group("col", c, NC, lambda peer: l_send, lbuf, s_l)
+    send_group("row", r, NR, lambda peer: hom.at[pl.ds(16 * peer, 16)], xa, s_x)
     lbuf[c] = l_send[...]
 
     loads["coup"].wait()
@@ -225,7 +216,6 @@
     b_send[...] = mm(tile.astype(BF), place).astype(BF)
     send_group("col", c, NC, lambda peer: b_send, bb1, s_b1)
     bb1[c] = b_send[...]
-    send_group("row", r, NR, lambda peer: hom.at[pl.ds(16 * peer, 16)], xa, s_x)
     xa[r] = hom[pl.ds(pl.multiple_of(16 * r, 16), 16), :]
     loads["t1"].wait()
     loads["t2"].wait()
@@ -235,6 +225,11 @@
     coup_own = jnp.concatenate(
         [coup_f[pl.ds(4 * b + j, 8, stride=16), :] for j in range(4)], axis=0
     )
+
+    arrived(bb1, NC - 1, s_b1)
+    b2_send[...] = jnp.sum(bb1[...].astype(F32), axis=0).astype(BF)
+    send_group("row", r, NR, lambda peer: b2_send, bb2, s_b2)
+    bb2[r] = b2_send[...]
 
     loads["prod"].wait()
     arrived(lbuf, NC - 1, s_l)
@@ -266,11 +261,6 @@
     send_group("col", c, NC, lambda peer: tl_send, tlbuf, s_tl)
     tlbuf[c] = tl_send[...]
     send_group("branch", b, NB, lambda peer: midbuf.at[b], midbuf, s_mid)
-
-    arrived(bb1, NC - 1, s_b1)
-    b2_send[...] = jnp.sum(bb1[...].astype(F32), axis=0).astype(BF)
-    send_group("row", r, NR, lambda peer: b2_send, bb2, s_b2)
-    bb2[r] = b2_send[...]
 
     for name in ("wq", "wk", "wv", "wg"):
         loads[name].wait()

time: 47.8 us -> 41.6 us (0.87)
  Pallas kernels: 44.8 us -> 38.6 us
    pallas_call x1, Pallas kernels: 44.8 us -> 38.6 us  [per_device(): pl.pallas_call(kernel, out_shape=(jax.ShapeDtypeStruct((16, 2, 8, 64), BF...]
where the time goes in v5:
time: 41.6 us; the launch traced here: 41.4 us
  Pallas kernels  38.6 us (93%)
  local copies, waits for them, and re-layouts  2.1 us (5%)
  between operations  0.65 us (2%)
    pallas_call x1, Pallas kernels, per_device(): pl.pallas_call(kernel, out_shape=(jax.ShapeDtypeStruct((16, 2, 8, 64), BF...  38.6 us
    unnamed x4, local copies, waits for them, and re-layouts  2.1 us

profile of v5, /device:TPU:1, one launch (start us, length us, event | category | flops | bytes accessed | tf_op | source)
XLA Modules:
  0.0 41.4 jit_solution(7212620540736479114)
XLA Ops:
  0.6 38.6 %block.1 = (bf16[16,2,8,64]{3,2,1,0:T(8,128)(2,1)}, bf16[8,16,128]{2,1,0:T(8,128)(2,1)}) custom-call(bf16[256,256]{1,0:T(8,128)(2,1)} %bitcast.12, bf16[128,128]{1,0:T(8,128)(2,1)} %bitcast.14, bf16[64,256]{1,0:T(8,128)(2,1)} %bitcast.15, bf16[64,256]{1,0:T(8,128)(2,1)} %bitcast.16, bf16[64,256]{1,0:T(8,128)(2,1)} %bitcast.17, bf16[64,256]{1,0:T(8,128)(2,1)} %bitcast.18, ...), custom_call_target="tpu_custom_call" | custom-call | tf_op jit(solution)/shard_map/block/pallas_call | solution.py:473
  39.3 0.0 copy-start
  39.3 1.5 %copy.19 = bf16[32,8,64]{2,1,0:T(8,128)(2,1)} copy(bf16[32,8,64]{2,1,0:T(8,128)(2,1)} %bitcast.13) | data formatting | bytes 65536
  40.8 0.0 copy-done
  40.8 0.6 %copy.20 = bf16[8,16,128]{2,1,0:T(8,128)(2,1)} copy(bf16[8,16,128]{2,1,0:T(8,128)(2,1)S(1)} %copy-done) | data formatting | bytes 65536
Async XLA Ops:
  39.3 1.5 %copy-start = (bf16[8,16,128]{2,1,0:T(8,128)(2,1)S(1)}, bf16[8,16,128]{2,1,0:T(8,128)(2,1)}, u32[]{:S(2)}) copy-start(bf16[8,16,128]{2,1,0:T(8,128)(2,1)} %get-tuple-element.9) | copy-start | bytes 98308

commit v6 on v5

--- a/solution.py
+++ b/solution.py
@@ -391,6 +391,21 @@
     for i in range(8):
         pair_out[i] = tile_f[pl.ds(i, 16, stride=8), :].astype(BF)
     left_device(pbuf, NB - 1, s_p)
+
+
+def hand_over(*arrays):
+    def kernel(*refs):
+        for n in range(len(arrays)):
+            refs[len(arrays) + n][...] = refs[n][...]
+
+    vmem = pl.BlockSpec(memory_space=pltpu.VMEM)
+    return pl.pallas_call(
+        kernel,
+        out_shape=tuple(jax.ShapeDtypeStruct(a.shape, a.dtype) for a in arrays),
+        in_specs=[vmem] * len(arrays),
+        out_specs=(vmem,) * len(arrays),
+        name="hand_over",
+    )(*arrays)
 
 
 def per_device(
@@ -486,7 +501,7 @@
         ),
         name="block",
     )(*operands)
-    return (msa.reshape(32, 8, 64), pairwise)
+    return hand_over(msa.reshape(32, 8, 64), pairwise)
 
 
 def solution(mesh):

time: 41.6 us -> 41 us (0.986)
  local copies, waits for them, and re-layouts: 2.1 us -> 0 us
  Pallas kernels: 38.6 us -> 40.1 us
    unnamed x4 -> x0, local copies, waits for them, and re-layouts: 2.1 us -> none
    pallas_call x0 -> x1, Pallas kernels: none -> 1.49 us  [hand_over(): pl.pallas_call(kernel, out_shape=tuple((jax.ShapeDtypeStruct(a.shape, a.d...]
where the time goes in v6:
time: 41 us; the launch traced here: 40.8 us
  Pallas kernels  40.1 us (98%)
  between operations  0.64 us (2%)
    pallas_call x1, Pallas kernels, per_device(): pl.pallas_call(kernel, out_shape=(jax.ShapeDtypeStruct((16, 2, 8, 64), BF...  38.7 us
    pallas_call x1, Pallas kernels, hand_over(): pl.pallas_call(kernel, out_shape=tuple((jax.ShapeDtypeStruct(a.shape, a.d...  1.49 us

profile of v6, /device:TPU:1, one launch (start us, length us, event | category | flops | bytes accessed | tf_op | source)
XLA Modules:
  0.0 40.8 jit_solution(12063644955707492695)
XLA Ops:
  0.6 38.7 %block.1 = (bf16[16,2,8,64]{3,2,1,0:T(8,128)(2,1)}, bf16[8,16,128]{2,1,0:T(8,128)(2,1)}) custom-call(bf16[256,256]{1,0:T(8,128)(2,1)} %bitcast.12, bf16[128,128]{1,0:T(8,128)(2,1)} %bitcast.14, bf16[64,256]{1,0:T(8,128)(2,1)} %bitcast.15, bf16[64,256]{1,0:T(8,128)(2,1)} %bitcast.16, bf16[64,256]{1,0:T(8,128)(2,1)} %bitcast.17, bf16[64,256]{1,0:T(8,128)(2,1)} %bitcast.18, ...), custom_call_target="tpu_custom_call" | custom-call | tf_op jit(solution)/shard_map/block/pallas_call | solution.py:488
  39.3 1.5 %hand_over.1 = (bf16[32,8,64]{2,1,0:T(8,128)(2,1)}, bf16[8,16,128]{2,1,0:T(8,128)(2,1)}) custom-call(bf16[32,8,64]{2,1,0:T(8,128)(2,1)} %bitcast.13, bf16[8,16,128]{2,1,0:T(8,128)(2,1)} %get-tuple-element.5.refs_1_), custom_call_target="tpu_custom_call" | custom-call | tf_op jit(solution)/shard_map/hand_over/pallas_call | solution.py:402

commit v7 on v6

--- a/solution.py
+++ b/solution.py
@@ -29,6 +29,10 @@
 
 def mm_tn(a, b):
     return lax.dot_general(a, b, (((0,), (0,)), ((), ())), preferred_element_type=F32)
+
+
+def farthest_first(size):
+    return sorted(range(size), key=lambda d: -min(d, size - d))
 
 
 def iota(shape, dim):
@@ -137,7 +141,7 @@
     pl.semaphore_wait(barrier, 15 + 7 + 3 + jnp.where(same_col, 15, 16))
 
     def send_group(axis, me, size, source, dest, sems):
-        def body(d, _):
+        for d in farthest_first(size)[:-1]:
             peer = wrapped(me + d, size)
             pltpu.make_async_remote_copy(
                 src_ref=source(peer),
@@ -147,19 +151,13 @@
                 device_id={axis: peer},
                 device_id_type=MESH,
             ).start()
-            return 0
-
-        lax.fori_loop(1, size, body, 0)
 
     def for_transposed(body):
-        def step(peer, _):
-            @pl.when(jnp.logical_or(peer != r, jnp.logical_not(same_col)))
-            def _():
-                body(peer)
-
-            return 0
-
-        lax.fori_loop(0, NR, step, 0)
+        for d in farthest_first(NR):
+            if d:
+                body(wrapped(r + d, NR))
+            else:
+                pl.when(jnp.logical_not(same_col))(lambda: body(r))
 
     def send_transposed(source, dest, sems):
         def send(peer):
@@ -343,22 +341,25 @@
     tlf[...] = tlbuf[...].astype(F32)
     trf[...] = trbuf[...].astype(F32)
 
-    def product_step(k, acc):
-        acc = list(acc)
-        for kk in range(4):
-            t = tlf[k, 8 * kk : 8 * kk + 8, :]
-            for j in range(16):
-                row = 8 * kk + j % 8
-                acc[j] = acc[j] + t * trf[j // 8, k, row : row + 1, :]
-        return tuple(acc)
-
-    product = lax.fori_loop(
-        0, NC, product_step, tuple(jnp.zeros((8, 128), F32) for _ in range(16))
-    )
-    product = jnp.concatenate(product, axis=0)
-    p_send[...] = product.astype(BF)
-    send_group("branch", b, NB, lambda peer: p_send, pbuf, s_p)
-    pbuf[b] = p_send[...]
+    for half_j in range(2):
+
+        def product_step(k, acc):
+            acc = list(acc)
+            for kk in range(4):
+                t = tlf[k, 8 * kk : 8 * kk + 8, :]
+                for j in range(8):
+                    row = 8 * kk + j
+                    acc[j] = acc[j] + t * trf[half_j, k, row : row + 1, :]
+            return tuple(acc)
+
+        product = lax.fori_loop(
+            0, NC, product_step, tuple(jnp.zeros((8, 128), F32) for _ in range(8))
+        )
+        p_send[half_j] = jnp.concatenate(product, axis=0).astype(BF)
+        send_group(
+            "branch", b, NB, lambda peer: p_send.at[half_j], pbuf.at[half_j], s_p.at[half_j]
+        )
+        pbuf[half_j, b] = p_send[half_j]
 
     wait_bytes(cb, s_c.at[1])
     ctx = cb[...].astype(F32).reshape(4, 128, 128)
@@ -384,13 +385,15 @@
     for n in range(NB):
         left_device(cb.at[n], NR if n else NR - 1, s_c)
 
-    arrived(pbuf, NB - 1, s_p)
-    total = jnp.sum(pbuf[...].astype(F32), axis=0)
+    for half_j in range(2):
+        arrived(pbuf.at[half_j], NB - 1, s_p.at[half_j])
+    total = jnp.sum(pbuf[...].astype(F32), axis=1).reshape(128, 128)
     change = mm(standardise(total).astype(BF), w_change[...])
     tile_f[...] = mid_all + closing * change
     for i in range(8):
         pair_out[i] = tile_f[pl.ds(i, 16, stride=8), :].astype(BF)
-    left_device(pbuf, NB - 1, s_p)
+    for half_j in range(2):
+        left_device(pbuf.at[half_j], NB - 1, s_p.at[half_j])
 
 
 def hand_over(*arrays):
@@ -475,8 +478,8 @@
         ((2, 8, 32, 128), BF),
         ((8, 32, 128), F32),
         ((2, 8, 32, 128), F32),
-        ((128, 128), BF),
-        ((4, 128, 128), BF),
+        ((2, 64, 128), BF),
+        ((2, 4, 64, 128), BF),
         ((128, 128), F32),
         ((16, 8, 128), BF),
         ((4, 16, 8, 128), BF),
@@ -495,7 +498,8 @@
         out_specs=(vmem, vmem),
         scratch_shapes=[pltpu.VMEM(*s) for s in scratch]
         + [pltpu.SemaphoreType.DMA((len(operands),))]
-        + [pltpu.SemaphoreType.DMA((2,))] * 12,
+        + [pltpu.SemaphoreType.DMA((2,))] * 11
+        + [pltpu.SemaphoreType.DMA((2, 2))],
         compiler_params=pltpu.CompilerParams(
             collective_id=0, has_side_effects=True
         ),

time: 41 us -> 41.2 us (level)
  no operation moved by 1% of the time
where the time goes in v7:
time: 41.2 us; the launch traced here: 41 us
  Pallas kernels  40.4 us (98%)
  between operations  0.64 us (2%)
    pallas_call x1, Pallas kernels, per_device(): pl.pallas_call(kernel, out_shape=(jax.ShapeDtypeStruct((16, 2, 8, 64), BF...  38.9 us
    pallas_call x1, Pallas kernels, hand_over(): pl.pallas_call(kernel, out_shape=tuple((jax.ShapeDtypeStruct(a.shape, a.d...  1.49 us

profile of v7, /device:TPU:1, one launch (start us, length us, event | category | flops | bytes accessed | tf_op | source)
XLA Modules:
  0.0 41.0 jit_solution(8193638947241860125)
XLA Ops:
  0.6 38.9 %block.1 = (bf16[16,2,8,64]{3,2,1,0:T(8,128)(2,1)}, bf16[8,16,128]{2,1,0:T(8,128)(2,1)}) custom-call(bf16[256,256]{1,0:T(8,128)(2,1)} %bitcast.12, bf16[128,128]{1,0:T(8,128)(2,1)} %bitcast.14, bf16[64,256]{1,0:T(8,128)(2,1)} %bitcast.15, bf16[64,256]{1,0:T(8,128)(2,1)} %bitcast.16, bf16[64,256]{1,0:T(8,128)(2,1)} %bitcast.17, bf16[64,256]{1,0:T(8,128)(2,1)} %bitcast.18, ...), custom_call_target="tpu_custom_call" | custom-call | tf_op jit(solution)/shard_map/block/pallas_call | solution.py:491
  39.5 1.5 %hand_over.1 = (bf16[32,8,64]{2,1,0:T(8,128)(2,1)}, bf16[8,16,128]{2,1,0:T(8,128)(2,1)}) custom-call(bf16[32,8,64]{2,1,0:T(8,128)(2,1)} %bitcast.13, bf16[8,16,128]{2,1,0:T(8,128)(2,1)} %get-tuple-element.5.refs_1_), custom_call_target="tpu_custom_call" | custom-call | tf_op jit(solution)/shard_map/hand_over/pallas_call | solution.py:405
